TPU v7x, 32 devices: a whole 2x2x4 slice. The times are simulated.
32 devices in a mesh: dp: 8 (over y, x, core), tensor: 4 (over z).
Axes of the slice: x: 2, y: 2, z: 4, core: 2. Of those that a mesh axis runs over, the one named last changes fastest.
Arguments:
- tokens: float32 [4864, 1024], P(('dp', 'tensor')), may hold values from -6 to 6
- counts: int32 [8], P('dp'), may hold values from 457 to 577, as said below
- vectors: float32 [8, 1024], P(None, ('dp', 'tensor')), may hold values from -2 to 3, as said below
- fc1_bias: float32 [4096], P(('dp', 'tensor')), may hold values from -4 to 4
- w_qkv: bfloat16 [3, 1024, 1024], P(None, 'dp', 'tensor'), may hold values from -0.1875 to 0.1875
- w_out: bfloat16 [1024, 1024], P('tensor', 'dp'), may hold values from -2.5 to 2.5
- w_fc1: bfloat16 [1024, 4096], P('dp', 'tensor'), may hold values from -0.1875 to 0.1875
- w_fc2: bfloat16 [4096, 1024], P('tensor', 'dp'), may hold values from -0.09375 to 0.09375
- cotangent: float32 [4864, 1024], P(('dp', 'tensor')), may hold values from -6 to 6
Outputs:
- layer_out: float32 [4864, 1024], P(('dp', 'tensor'))
- input_grad: float32 [4864, 1024], P(('dp', 'tensor'))
- vectors_grad: float32 [8, 1024], P(None, ('dp', 'tensor'))
- fc1_bias_grad: float32 [4096], P(('dp', 'tensor'))
- qkv_grad: float32 [3, 1024, 1024], P(None, 'dp', 'tensor')
- out_grad: float32 [1024, 1024], P('tensor', 'dp')
- fc1_grad: float32 [1024, 4096], P('dp', 'tensor')
- fc2_grad: float32 [4096, 1024], P('tensor', 'dp')
Inputs may be any that keep to these rules, and one draw needn't show every extreme that they name: `counts`: an image's valid tokens are its first ones; some image has exactly 577. `vectors`: rows 0 and 5 are gains near 1; the other rows are biases.
All inputs are finite; a program needn't handle non-finite values.
Results may differ from a plain program's by a relative error of at most 0.017.
Values may be sent and summed in bfloat16 or wider, within the bound.
A program may use at most 128 MiB of HBM per device.

v0:
```python
import jax
import jax.numpy as jnp
from jax import lax
from jax.sharding import PartitionSpec as P

HEAD_DIM = 64


EPSILON = 1e-06
NEGATIVE = -1e30


def layer_norm(values, gain, shift):
    centred = values - jnp.mean(values, axis=-1, keepdims=True)
    spread = jnp.mean(centred * centred, axis=-1, keepdims=True)
    return centred * lax.rsqrt(spread + EPSILON) * gain + shift


def exact_gelu(values):
    return jax.nn.gelu(values, approximate=False)


def masked_scores(query, keys, valid_keys, scale):
    scores = jnp.einsum("qhd,khd->hqk", query, keys, preferred_element_type=jnp.float32) * scale
    return jnp.where(valid_keys[None, None, :], scores, NEGATIVE)


def attend(query, keys, values, valid_keys, scale):
    scores = masked_scores(query, keys, valid_keys, scale)
    largest = jnp.max(scores, axis=-1, keepdims=True)
    powers = jnp.exp(scores - largest)
    total = jnp.sum(powers, axis=-1, keepdims=True)
    probs = (powers / total).astype(jnp.bfloat16)
    mixed = jnp.einsum("hqk,khd->qhd", probs, values, preferred_element_type=jnp.float32)
    return (mixed, largest + jnp.log(total))


def attend_back(query, keys, values, valid_keys, scale, log_total, grad_mixed):
    scores = masked_scores(query, keys, valid_keys, scale)
    probs = jnp.exp(scores - log_total)
    grad_probs = jnp.einsum("qhd,khd->hqk", grad_mixed, values, preferred_element_type=jnp.float32)
    inner = jnp.sum(grad_probs * probs, axis=-1, keepdims=True)
    grad_scores = (probs * (grad_probs - inner)).astype(jnp.bfloat16)
    grad_values = jnp.einsum(
        "hqk,qhd->khd", probs.astype(jnp.bfloat16), grad_mixed, preferred_element_type=jnp.float32
    )
    grad_query = (
        jnp.einsum("hqk,khd->qhd", grad_scores, keys, preferred_element_type=jnp.float32) * scale
    )
    grad_keys = (
        jnp.einsum("hqk,qhd->khd", grad_scores, query, preferred_element_type=jnp.float32) * scale
    )
    return (grad_query, grad_keys, grad_values)


def on_device(tokens, counts, vectors, fc1_bias, w_qkv, w_out, w_fc1, w_fc2, cotangent):
    full_vectors, full_fc1 = (
        lax.all_gather(vectors, ("dp", "tensor"), axis=1, tiled=True),
        lax.all_gather(fc1_bias, ("dp", "tensor"), axis=0, tiled=True),
    )
    qkv_all, out_all, fc1_all, fc2_all = (
        lax.all_gather(w_qkv, "dp", axis=1, tiled=True),
        lax.all_gather(w_out, "dp", axis=1, tiled=True),
        lax.all_gather(w_fc1, "dp", axis=0, tiled=True),
        lax.all_gather(w_fc2, "dp", axis=1, tiled=True),
    )
    tensor_count = lax.axis_size("tensor")
    tensor_index = lax.axis_index("tensor")
    local_rows = tokens.shape[0]
    block_rows = local_rows * tensor_count
    images = counts.shape[0]
    seq = block_rows // images
    width = qkv_all.shape[2]
    model_width = qkv_all.shape[1]
    hidden_width = fc1_all.shape[1]
    heads_local = width // HEAD_DIM
    scale = HEAD_DIM ** (-0.5)
    places = jnp.arange(block_rows, dtype=jnp.int32)
    owner = places // seq
    position = places - owner * seq
    picks = owner[:, None] == jnp.arange(images, dtype=jnp.int32)[None, :]
    row_count = jnp.sum(jnp.where(picks, counts[None, :], 0), axis=1)
    block_valid = position < row_count
    local_valid = lax.dynamic_slice_in_dim(block_valid, tensor_index * local_rows, local_rows)
    local_valid = local_valid.astype(jnp.float32)[:, None]
    query_bias = lax.dynamic_slice_in_dim(full_vectors[2], tensor_index * width, width)
    value_bias = lax.dynamic_slice_in_dim(full_vectors[3], tensor_index * width, width)
    hidden_bias = lax.dynamic_slice_in_dim(full_fc1, tensor_index * hidden_width, hidden_width)
    normed = layer_norm(tokens, full_vectors[0], full_vectors[1]).astype(jnp.bfloat16)
    gathered = lax.all_gather(normed, "tensor", axis=0, tiled=True)
    projected = jnp.einsum("rd,kde->kre", gathered, qkv_all, preferred_element_type=jnp.float32)
    query = (
        (projected[0] + query_bias).astype(jnp.bfloat16).reshape(block_rows, heads_local, HEAD_DIM)
    )
    keys = projected[1].astype(jnp.bfloat16).reshape(block_rows, heads_local, HEAD_DIM)
    values = (
        (projected[2] + value_bias).astype(jnp.bfloat16).reshape(block_rows, heads_local, HEAD_DIM)
    )
    mixed_one, total_one = attend(query, keys, values, block_valid, scale)
    mixed_all = mixed_one.reshape(block_rows, width).astype(jnp.bfloat16)
    attn_part = jnp.dot(mixed_all, out_all, preferred_element_type=jnp.float32)
    attn_local = lax.psum_scatter(
        attn_part.astype(jnp.bfloat16), "tensor", scatter_dimension=0, tiled=True
    ).astype(jnp.float32)
    middle = tokens + local_valid * (attn_local + full_vectors[4])
    normed2 = layer_norm(middle, full_vectors[5], full_vectors[6]).astype(jnp.bfloat16)
    gathered2 = lax.all_gather(normed2, "tensor", axis=0, tiled=True)
    pre = jnp.dot(gathered2, fc1_all, preferred_element_type=jnp.float32) + hidden_bias
    hidden_float, gelu_back = jax.vjp(exact_gelu, pre)
    hidden = hidden_float.astype(jnp.bfloat16)
    mlp_part = jnp.dot(hidden, fc2_all, preferred_element_type=jnp.float32)
    mlp_local = lax.psum_scatter(
        mlp_part.astype(jnp.bfloat16), "tensor", scatter_dimension=0, tiled=True
    ).astype(jnp.float32)
    layer_out = middle + local_valid * (mlp_local + full_vectors[7])
    masked_out = local_valid * cotangent
    grad_shift2 = jnp.sum(masked_out, axis=0)
    gathered_grad = lax.all_gather(masked_out.astype(jnp.bfloat16), "tensor", axis=0, tiled=True)
    fc2_term = jnp.einsum("rf,rd->fd", hidden, gathered_grad, preferred_element_type=jnp.float32)
    grad_hidden = jnp.einsum(
        "rd,fd->rf", gathered_grad, fc2_all, preferred_element_type=jnp.float32
    )
    grad_pre = gelu_back(grad_hidden)[0].astype(jnp.bfloat16)
    hidden_bias_grad = jnp.sum(grad_pre.astype(jnp.float32), axis=0)
    fc1_term = jnp.einsum("rd,rf->df", gathered2, grad_pre, preferred_element_type=jnp.float32)
    normed2_part = jnp.einsum("rf,df->rd", grad_pre, fc1_all, preferred_element_type=jnp.float32)
    grad_normed2 = lax.psum_scatter(
        normed2_part.astype(jnp.bfloat16), "tensor", scatter_dimension=0, tiled=True
    ).astype(jnp.float32)
    second_norm, second_back = jax.vjp(layer_norm, middle, full_vectors[5], full_vectors[6])
    grad_through, gain2_grad, shift2_grad = second_back(grad_normed2)
    grad_middle = cotangent + grad_through
    masked_middle = local_valid * grad_middle
    out_bias_grad = jnp.sum(masked_middle, axis=0)
    gathered_attn = lax.all_gather(masked_middle.astype(jnp.bfloat16), "tensor", axis=0, tiled=True)
    out_term = jnp.einsum("re,rd->ed", mixed_all, gathered_attn, preferred_element_type=jnp.float32)
    grad_mixed = jnp.einsum("rd,ed->re", gathered_attn, out_all, preferred_element_type=jnp.float32)
    grad_mixed = grad_mixed.astype(jnp.bfloat16).reshape(block_rows, heads_local, HEAD_DIM)
    grad_q, grad_k, grad_v = attend_back(
        query, keys, values, block_valid, scale, total_one, grad_mixed
    )
    grad_query = grad_q.reshape(block_rows, width).astype(jnp.bfloat16)
    grad_keys = grad_k.reshape(block_rows, width).astype(jnp.bfloat16)
    grad_values = grad_v.reshape(block_rows, width).astype(jnp.bfloat16)
    stacked = jnp.stack([grad_query, grad_keys, grad_values])
    query_bias_grad = jnp.sum(grad_query.astype(jnp.float32), axis=0)
    value_bias_grad = jnp.sum(grad_values.astype(jnp.float32), axis=0)
    qkv_term = jnp.einsum("rd,kre->kde", gathered, stacked, preferred_element_type=jnp.float32)
    normed_part = jnp.einsum("kre,kde->rd", stacked, qkv_all, preferred_element_type=jnp.float32)
    qkv_grad, out_grad, fc1_grad, fc2_grad = (
        lax.psum_scatter(qkv_term, "dp", scatter_dimension=1, tiled=True),
        lax.psum_scatter(out_term, "dp", scatter_dimension=1, tiled=True),
        lax.psum_scatter(fc1_term, "dp", scatter_dimension=0, tiled=True),
        lax.psum_scatter(fc2_term, "dp", scatter_dimension=1, tiled=True),
    )
    grad_normed = lax.psum_scatter(
        normed_part.astype(jnp.bfloat16), "tensor", scatter_dimension=0, tiled=True
    ).astype(jnp.float32)
    first_norm, first_back = jax.vjp(layer_norm, tokens, full_vectors[0], full_vectors[1])
    grad_input_norm, gain1_grad, shift1_grad = first_back(grad_normed)
    input_grad = grad_middle + grad_input_norm
    zeros_model = jnp.zeros((model_width,), jnp.float32)
    query_bias_full = lax.dynamic_update_slice_in_dim(
        zeros_model, query_bias_grad, tensor_index * width, 0
    )
    value_bias_full = lax.dynamic_update_slice_in_dim(
        zeros_model, value_bias_grad, tensor_index * width, 0
    )
    vector_terms = jnp.stack(
        [
            gain1_grad,
            shift1_grad,
            query_bias_full,
            value_bias_full,
            out_bias_grad,
            gain2_grad,
            shift2_grad,
            grad_shift2,
        ]
    )
    zeros_hidden = jnp.zeros((full_fc1.shape[0],), jnp.float32)
    hidden_bias_full = lax.dynamic_update_slice_in_dim(
        zeros_hidden, hidden_bias_grad, tensor_index * hidden_width, 0
    )
    vectors_grad, fc1_bias_grad = (
        lax.psum_scatter(vector_terms, ("dp", "tensor"), scatter_dimension=1, tiled=True),
        lax.psum_scatter(hidden_bias_full, ("dp", "tensor"), scatter_dimension=0, tiled=True),
    )
    return (
        layer_out,
        input_grad,
        vectors_grad,
        fc1_bias_grad,
        qkv_grad,
        out_grad,
        fc1_grad,
        fc2_grad,
    )


def solution(mesh):
    placed = (
        P(("dp", "tensor"), None),
        P("dp"),
        P(None, ("dp", "tensor")),
        P(("dp", "tensor")),
        P(None, "dp", "tensor"),
        P("tensor", "dp"),
        P("dp", "tensor"),
        P("tensor", "dp"),
        P(("dp", "tensor"), None),
    )
    return jax.shard_map(
        on_device,
        mesh=mesh,
        in_specs=placed,
        out_specs=(
            P(("dp", "tensor"), None),
            P(("dp", "tensor"), None),
            P(None, ("dp", "tensor")),
            P(("dp", "tensor")),
            P(None, "dp", "tensor"),
            P("tensor", "dp"),
            P("dp", "tensor"),
            P("tensor", "dp"),
        ),
        check_vma=False,
    )
```

profile of v0, /device:TPU:0, one launch (start us, length us, event | category | flops | bytes accessed | tf_op | source)
XLA Modules:
  0.0 803.0 jit_solution(1147985467904251428)
XLA Ops:
  7.2 1.2 reduce_sum.167
  8.4 1.3 multiply_reduce_fusion.2
  9.8 70.9 %all-gather = f32[32,32,8]{1,2,0:T(8,128)S(1)} all-gather(f32[1,32,8]{1,2,0:T(8,128)} %bitcast.114), channel_id=1, replica_groups=mesh['dp'=8,'tensor'=4] {'dp','tensor'}, dimensions={0}, use_global_device_ids=true | all-gather | bytes 33792 | tf_op jit(solution)/shard_map/all_gather | solution.py:58
  80.8 2.0 add_convert_fusion.4
  82.9 0.7 all-gather.12.cloned.1.call-update
  84.5 9.0 %all_gather.33 = bf16[256,1024]{1,0:T(8,128)(2,1)S(1)} all-gather(bf16[256,128]{1,0:T(8,128)(2,1)S(1)} %copy-done.9), channel_id=1, replica_groups=mesh['dp'=8,'tensor'=4] {'dp'}, dimensions={1}, use_global_device_ids=true | all-gather | bytes 589824 | tf_op jit(solution)/shard_map/all_gather | solution.py:63
  93.5 17.3 %all-gather.10.cloned.1.call-done = bf16[608,1024]{1,0:T(8,128)(2,1)} async-done(((bf16[152,1024]{1,0:T(8,128)(2,1)}), bf16[608,1024]{1,0:T(8,128)(2,1)}) %all-gather.10.cloned.1.call-update) | async-done | bytes 1245200 | tf_op jit(solution)/shard_map/all_gather | solution.py:90
  110.8 26.7 %all-gather.12.cloned.1.call-done = bf16[3,1024,256]{2,1,0:T(8,128)(2,1)} async-done(((bf16[3,128,256]{2,1,0:T(8,128)(2,1)}), bf16[3,1024,256]{2,1,0:T(8,128)(2,1)}) %all-gather.12.cloned.1.call-update) | async-done | bytes 1572880 | tf_op jit(solution)/shard_map/all_gather | solution.py:62
  137.5 2.9 convolution_bitcast_fusion.1
  141.3 1.6 fusion.42
  142.9 0.9 fusion
  143.8 1.7 copy-done
  145.5 1.2 fusion.19
  146.8 0.7 copy-done.5
  147.5 1.6 convolution_convert_fusion
  149.8 29.6 %reduce-scatter.12.cloned.1.call-done = bf16[152,1024]{1,0:T(8,128)(2,1)} async-done(((bf16[608,1024]{1,0:T(8,128)(2,1)}), bf16[152,1024]{1,0:T(8,128)(2,1)}) %reduce-scatter.12.cloned.1.call-update) | async-done | bytes 311312 | tf_op jit(solution)/shard_map/reduce_scatter | solution.py:102
  179.4 1.9 fusion.39
  181.5 0.9 add_convert_fusion.3
  183.1 0.7 all-gather.20.cloned.1.call-update
  183.8 66.0 %all-gather.1 = f32[32,1,128]{2,1,0:T(1,128)S(1)} all-gather(f32[1,1,128]{2,1,0:T(1,128)} %bitcast.115), channel_id=1, replica_groups=mesh['dp'=8,'tensor'=4] {'dp','tensor'}, dimensions={0}, use_global_device_ids=true | all-gather | bytes 16896 | tf_op jit(solution)/shard_map/all_gather | solution.py:59
  249.8 5.0 fusion.43
  254.8 16.1 %all-gather.18.cloned.1.call-done = bf16[1024,1024]{1,0:T(8,128)(2,1)} async-done(((bf16[1024,128]{1,0:T(8,128)(2,1)}), bf16[1024,1024]{1,0:T(8,128)(2,1)}) %all-gather.18.cloned.1.call-update) | async-done | bytes 2097168 | tf_op jit(solution)/shard_map/all_gather | solution.py:65
  271.0 33.8 %all-gather.20.cloned.1.call-done = bf16[608,1024]{1,0:T(8,128)(2,1)} async-done(((bf16[152,1024]{1,0:T(8,128)(2,1)}), bf16[608,1024]{1,0:T(8,128)(2,1)}) %all-gather.20.cloned.1.call-update) | async-done | bytes 1245200 | tf_op jit(solution)/shard_map/all_gather | solution.py:118
  304.8 11.0 %convert_reduce_fusion = (f32[1024]{0:T(1024)}, bf16[608,1024]{1,0:T(8,128)(2,1)S(1)}, f32[608,1024]{1,0:T(8,128)}) fusion(f32[608,1024]{1,0:T(8,128)} %fusion.43, f32[1024]{0:T(1024)S(1)} %dynamic_slice.15, bf16[608,1024]{1,0:T(8,128)(2,1)} %all-gather.20.cloned.1.call-done, bf16[1024,1024]{1,0:T(8,128)(2,1)} %all-gather.18.cloned.1.call-done), kind=kOutput, calls=%fused_computation.14 | convolution fusion | flops 1321761792 | bytes 9576448 | tf_op jit(solution)/shard_map/rd,fd->rf/dot_general | solution.py:120
  315.7 1.1 copy-done.30
  316.8 2.6 convolution_convert_fusion.1
  319.5 3.2 multiply_convert_fusion.1
  322.7 1.0 copy-done.8
  323.7 2.5 convolution_convert_fusion.2
  326.3 22.5 %reduce-scatter.16.cloned.1.call-done = bf16[152,1024]{1,0:T(8,128)(2,1)} async-done(((bf16[608,1024]{1,0:T(8,128)(2,1)}), bf16[152,1024]{1,0:T(8,128)(2,1)}) %reduce-scatter.16.cloned.1.call-update) | async-done | bytes 311312 | tf_op jit(solution)/shard_map/reduce_scatter | solution.py:127
  348.8 1.8 convert_reduce_fusion.2
  350.7 2.0 fusion.26
  353.2 26.9 %reduce-scatter.14.cloned.1.call-done = bf16[152,1024]{1,0:T(8,128)(2,1)} async-done(((bf16[608,1024]{1,0:T(8,128)(2,1)}), bf16[152,1024]{1,0:T(8,128)(2,1)}) %reduce-scatter.14.cloned.1.call-update) | async-done | bytes 311312 | tf_op jit(solution)/shard_map/reduce_scatter | solution.py:112
  380.1 3.1 multiply_reduce_fusion.4
  383.3 0.8 multiply_convert_fusion.2
  384.4 30.2 %all-gather.22.cloned.1.call-done = bf16[608,1024]{1,0:T(8,128)(2,1)} async-done(((bf16[152,1024]{1,0:T(8,128)(2,1)}), bf16[608,1024]{1,0:T(8,128)(2,1)}) %all-gather.22.cloned.1.call-update) | async-done | bytes 1245200 | tf_op jit(solution)/shard_map/all_gather | solution.py:135
  414.6 1.9 convolution_convert_fusion.3
  416.7 4.7 convert_reduce_fusion.3
  421.4 4.4 multiply_reduce_fusion
  425.8 1.3 multiply_convert_fusion
  427.1 1.1 fusion.15
  428.2 0.7 convert_reduce_fusion.4
  429.5 3.6 bitcast_convert_fusion
  433.4 29.1 %reduce-scatter.18.cloned.1.call-done = bf16[152,1024]{1,0:T(8,128)(2,1)} async-done(((bf16[608,1024]{1,0:T(8,128)(2,1)}), bf16[152,1024]{1,0:T(8,128)(2,1)}) %reduce-scatter.18.cloned.1.call-update) | async-done | bytes 311312 | tf_op jit(solution)/shard_map/reduce_scatter | solution.py:156
  462.6 1.2 convert_reduce_fusion.1
  463.9 1.4 fusion.27
  465.3 1.0 copy.61
  466.4 4.5 convolution_bitcast_fusion
  471.0 0.9 copy-done.6
  472.4 1.6 fusion.44
  474.0 5.4 fusion.46
  479.8 1.0 copy-done.29
  480.7 5.1 fusion.45
  485.9 0.6 copy-done.26
  486.7 39.2 %all-reduce = f32[4096]{0:T(1024)S(1)} all-reduce(f32[4096]{0:T(1024)S(1)} %dynamic_update_slice.13), channel_id=7, replica_groups=mesh['dp'=8,'tensor'=4] {'dp','tensor'}, use_global_device_ids=true, to_apply=%region_25.26.clone | all-reduce | flops 4096 | bytes 32768
  525.8 0.6 dynamic-slice.2
  526.4 1.1 add_add_fusion.2
  527.5 72.3 %reduce-scatter.28.cloned.1.call-done = f32[32,8]{1,0:T(8,128)} async-done(((f32[1024,8]{1,0:T(8,128)}), f32[32,8]{1,0:T(8,128)}) %reduce-scatter.28.cloned.1.call-update) | async-done | bytes 1040
  599.9 1.4 copy.62
  601.2 45.0 %reduce-scatter.20.cloned.1.call-done = f32[3,128,256]{1,2,0:T(8,128)} async-done(((f32[3,1024,256]{1,2,0:T(8,128)}), f32[3,128,256]{1,2,0:T(8,128)}) %reduce-scatter.20.cloned.1.call-update) | async-done | bytes 393232 | tf_op jit(solution)/shard_map/reduce_scatter | solution.py:151
  646.2 1.9 copy.56
  648.1 37.7 %reduce-scatter.22.cloned.1.call-done = f32[256,128]{1,0:T(8,128)} async-done(((f32[256,1024]{1,0:T(8,128)}), f32[256,128]{1,0:T(8,128)}) %reduce-scatter.22.cloned.1.call-update) | async-done | bytes 131088 | tf_op jit(solution)/shard_map/reduce_scatter | solution.py:152
  685.8 55.1 %reduce-scatter.26.cloned.1.call-done = f32[1024,128]{1,0:T(8,128)} async-done(((f32[1024,1024]{1,0:T(8,128)}), f32[1024,128]{1,0:T(8,128)}) %reduce-scatter.26.cloned.1.call-update) | async-done | bytes 524304 | tf_op jit(solution)/shard_map/reduce_scatter | solution.py:154
  741.0 55.5 %reduce-scatter.24.cloned.1.call-done = f32[128,1024]{1,0:T(8,128)} async-done(((f32[1024,1024]{1,0:T(8,128)}), f32[128,1024]{1,0:T(8,128)}) %reduce-scatter.24.cloned.1.call-update) | async-done | bytes 524304 | tf_op jit(solution)/shard_map/reduce_scatter | solution.py:153
  (130 shorter events, 6.2 us)
Async XLA Ops:
  7.2 77.4 %copy-start.9 = (bf16[256,128]{1,0:T(8,128)(2,1)S(1)}, bf16[256,128]{1,0:T(8,128)(2,1)}, u32[]{:S(2)}) copy-start(bf16[256,128]{1,0:T(8,128)(2,1)} %param.14) | copy-start | bytes 196612
  7.2 103.7 %all-gather.10.cloned.1.call-start = ((), (), s32[]{:S(2)}) async-start(), calls=%async_computation.9 | async-start | bytes 1556480 | tf_op jit(solution)/shard_map/all_gather | solution.py:90
  8.4 132.0 %copy-start.10 = (f32[152]{0:T(256)}, f32[152]{0:T(256)S(1)}, u32[]{:S(2)}) copy-start(f32[152]{0:T(256)S(1)} %broadcast_multiply_fusion.1) | copy-start | bytes 1828
  9.7 74.6 %copy-start.21 = (f32[152]{0:T(256)}, f32[152]{0:T(256)S(1)}, u32[]{:S(2)}) copy-start(f32[152]{0:T(256)S(1)} %multiply_reduce_fusion.2) | copy-start | bytes 1828
  9.8 130.7 %copy-start.18 = (f32[152]{0:T(256)}, f32[152]{0:T(256)S(1)}, u32[]{:S(2)}) copy-start(f32[152]{0:T(256)S(1)} %fusion.32) | copy-start | bytes 1828
  82.8 54.7 %all-gather.12.cloned.1.call-start = ((), (), s32[]{:S(2)}) async-start(), calls=%async_computation.10 | async-start | bytes 1769472 | tf_op jit(solution)/shard_map/all_gather | solution.py:62
  83.6 95.8 %reduce-scatter.12.cloned.1.call-start = ((), (), s32[]{:S(2)}) async-start(), calls=%async_computation.11 | async-start | bytes 1556480 | tf_op jit(solution)/shard_map/reduce_scatter | solution.py:102
  84.4 56.9 %copy-start.12 = (f32[4,64]{1,0:T(4,128)}, f32[4,64]{1,0:T(4,128)S(1)}, u32[]{:S(2)}) copy-start(f32[4,64]{1,0:T(4,128)S(1)} %add.162) | copy-start | bytes 3076
  84.5 59.2 %copy-start.24 = (f32[4,64]{1,0:T(4,128)}, f32[4,64]{1,0:T(4,128)S(1)}, u32[]{:S(2)}) copy-start(f32[4,64]{1,0:T(4,128)S(1)} %add.159) | copy-start | bytes 3076
  93.5 53.3 %copy-start.4 = (bf16[256,1024]{1,0:T(8,128)(2,1)}, bf16[256,1024]{1,0:T(8,128)(2,1)S(1)}, u32[]{:S(2)}) copy-start(bf16[256,1024]{1,0:T(8,128)(2,1)S(1)} %all_gather.33) | copy-start | bytes 1572868
  142.9 2.6 copy-start
  146.7 0.7 copy-start.5
  146.7 32.7 %copy-start.1 = (f32[152,1024]{1,0:T(8,128)S(1)}, f32[152,1024]{1,0:T(8,128)}, u32[]{:S(2)}) copy-start(f32[152,1024]{1,0:T(8,128)} %param.9) | copy-start | bytes 1867780
  146.8 32.6 %copy-start.3 = (f32[152,1024]{1,0:T(8,128)S(1)}, f32[152,1024]{1,0:T(8,128)}, u32[]{:S(2)}) copy-start(f32[152,1024]{1,0:T(8,128)} %param.17) | copy-start | bytes 1867780
  149.1 100.8 %all-gather.16.cloned.1.call-start = ((), (), s32[]{:S(2)}) async-start(), calls=%async_computation.13 | async-start | bytes 2359296 | tf_op jit(solution)/shard_map/all_gather | solution.py:64
  149.6 100.2 %all-gather.14.cloned.1.call-start = ((), (), s32[]{:S(2)}) async-start(), calls=%async_computation.12 | async-start | bytes 1556480 | tf_op jit(solution)/shard_map/all_gather | solution.py:107
  181.5 169.2 %copy-start.20 = (f32[152]{0:T(256)}, f32[152]{0:T(256)S(1)}, u32[]{:S(2)}) copy-start(f32[152]{0:T(256)S(1)} %fusion.33) | copy-start | bytes 1828
  182.4 88.5 %all-gather.18.cloned.1.call-start = ((), (), s32[]{:S(2)}) async-start(), calls=%async_computation.14 | async-start | bytes 2359296 | tf_op jit(solution)/shard_map/all_gather | solution.py:65
  183.0 121.8 %all-gather.20.cloned.1.call-start = ((), (), s32[]{:S(2)}) async-start(), calls=%async_computation.16 | async-start | bytes 1556480 | tf_op jit(solution)/shard_map/all_gather | solution.py:118
  183.8 165.1 %reduce-scatter.16.cloned.1.call-start = ((), (), s32[]{:S(2)}) async-start(), calls=%async_computation.17 | async-start | bytes 1556480 | tf_op jit(solution)/shard_map/reduce_scatter | solution.py:127
  304.8 12.0 %copy-start.27 = (bf16[1024,1024]{1,0:T(8,128)(2,1)S(1)}, bf16[1024,1024]{1,0:T(8,128)(2,1)}, u32[]{:S(2)}) copy-start(bf16[1024,1024]{1,0:T(8,128)(2,1)} %all-gather.16.cloned.1.call-done) | copy-start | bytes 6291460
  315.7 1.1 copy-start.30
  319.4 60.7 %reduce-scatter.14.cloned.1.call-start = ((), (), s32[]{:S(2)}) async-start(), calls=%async_computation.15 | async-start | bytes 1556480 | tf_op jit(solution)/shard_map/reduce_scatter | solution.py:112
  319.5 4.3 copy-start.28
  322.7 1.0 copy-start.8
  326.3 88.3 %all-gather.22.cloned.1.call-start = ((), (), s32[]{:S(2)}) async-start(), calls=%async_computation.18 | async-start | bytes 1556480 | tf_op jit(solution)/shard_map/all_gather | solution.py:135
  384.1 78.5 %reduce-scatter.18.cloned.1.call-start = ((), (), s32[]{:S(2)}) async-start(), calls=%async_computation.19 | async-start | bytes 1556480 | tf_op jit(solution)/shard_map/reduce_scatter | solution.py:156
  416.7 4.7 copy-start.25
  416.7 9.1 %slice-start = ((s8[6225920]{0:T(1024)(128)(4,1)}), s8[4194304]{0:T(1024)(128)(4,1)S(1)}, s32[]{:S(2)}) async-start(s8[6225920]{0:T(1024)(128)(4,1)} %bitcast.77), calls=%async_computation.25 | async-start | bytes 8388608
  421.4 4.4 slice-start.1
  425.8 1.3 copy-start.13
  429.5 3.8 copy-start.23
  429.5 33.1 %copy-start.11 = (f32[152]{0:T(256)S(1)}, f32[152]{0:T(256)}, u32[]{:S(2)}) copy-start(f32[152]{0:T(256)} %copy-done.10) | copy-start | bytes 1828
  429.5 34.3 %copy-start.22 = (f32[152]{0:T(256)S(1)}, f32[152]{0:T(256)}, u32[]{:S(2)}) copy-start(f32[152]{0:T(256)} %copy-done.21) | copy-start | bytes 1828
  429.5 34.3 %copy-start.19 = (f32[152]{0:T(256)S(1)}, f32[152]{0:T(256)}, u32[]{:S(2)}) copy-start(f32[152]{0:T(256)} %copy-done.18) | copy-start | bytes 1828
  433.1 32.1 %copy-start.14 = (f32[1024]{0:T(1024)S(1)}, f32[1024]{0:T(1024)}, u32[]{:S(2)}) copy-start(f32[1024]{0:T(1024)} %get-tuple-element.36) | copy-start | bytes 12292
  433.2 32.1 %copy-start.15 = (f32[1024]{0:T(1024)S(1)}, f32[1024]{0:T(1024)}, u32[]{:S(2)}) copy-start(f32[1024]{0:T(1024)} %get-tuple-element.40) | copy-start | bytes 12292
  433.2 32.1 %copy-start.16 = (f32[1024]{0:T(1024)S(1)}, f32[1024]{0:T(1024)}, u32[]{:S(2)}) copy-start(f32[1024]{0:T(1024)} %get-tuple-element.41) | copy-start | bytes 12292
  433.2 32.1 %copy-start.17 = (f32[1024]{0:T(1024)S(1)}, f32[1024]{0:T(1024)}, u32[]{:S(2)}) copy-start(f32[1024]{0:T(1024)} %get-tuple-element.32) | copy-start | bytes 12292
  433.2 166.7 %reduce-scatter.28.cloned.1.call-start = ((), (), s32[]{:S(2)}) async-start(), calls=%async_computation.24 | async-start | bytes 540672
  466.4 179.8 %reduce-scatter.20.cloned.1.call-start = ((), (), s32[]{:S(2)}) async-start(), calls=%async_computation.20 | async-start | bytes 3538944 | tf_op jit(solution)/shard_map/reduce_scatter | solution.py:151
  471.0 1.0 copy-start.6
  471.0 1.4 copy-start.7
  471.0 214.8 %reduce-scatter.22.cloned.1.call-start = ((), (), s32[]{:S(2)}) async-start(), calls=%async_computation.21 | async-start | bytes 1179648 | tf_op jit(solution)/shard_map/reduce_scatter | solution.py:152
  473.9 267.0 %reduce-scatter.26.cloned.1.call-start = ((), (), s32[]{:S(2)}) async-start(), calls=%async_computation.23 | async-start | bytes 4718592 | tf_op jit(solution)/shard_map/reduce_scatter | solution.py:154
  479.4 1.3 copy-start.29
  479.5 317.0 %reduce-scatter.24.cloned.1.call-start = ((), (), s32[]{:S(2)}) async-start(), calls=%async_computation.22 | async-start | bytes 4718592 | tf_op jit(solution)/shard_map/reduce_scatter | solution.py:153
  485.8 0.7 copy-start.26
  485.8 40.6 %copy-start.2 = (bf16[152,1024]{1,0:T(8,128)(2,1)S(1)}, bf16[152,1024]{1,0:T(8,128)(2,1)}, u32[]{:S(2)}) copy-start(bf16[152,1024]{1,0:T(8,128)(2,1)} %reduce-scatter.18.cloned.1.call-done) | copy-start | bytes 933892
Sparse Core Ops, SparseCore 0:
  83.0 27.8 all-gather.9
  112.7 24.7 all-gather.11
  149.2 30.1 reduce-scatter.11
  181.3 26.6 all-gather.15
  210.1 31.6 all-gather.13
  243.7 27.2 all-gather.17
  273.2 31.5 all-gather.19
  319.5 29.2 reduce-scatter.15
  351.2 28.9 reduce-scatter.13
  384.2 30.3 all-gather.21
  433.3 29.2 reduce-scatter.17
  466.5 133.2 reduce-scatter.27
  603.6 42.5 reduce-scatter.19
  649.8 35.9 reduce-scatter.21
  689.6 51.3 reduce-scatter.25
  745.1 51.3 reduce-scatter.23
where the time goes:
time: 804 us; the launch traced here: 803 us
  waiting for transfers between devices  501 us (62%)
  blocking collectives  185 us (23%)
  matrix products  61.4 us (8%)
  other arithmetic  25 us (3%)
  between operations  15.1 us (2%)
  local copies, waits for them, and re-layouts  14.8 us (2%)
    unnamed x17, waiting for transfers between devices  75 us
    all_gather x1, blocking collectives, on_device(): lax.all_gather(vectors, ('dp', 'tensor'), axis=1, tiled=True)  70.9 us
    all_gather x1, blocking collectives, on_device(): lax.all_gather(fc1_bias, ('dp', 'tensor'), axis=0, tiled=True)  66 us
    reduce_scatter x1, waiting for transfers between devices, on_device(): lax.psum_scatter(fc1_term, 'dp', scatter_dimension=0, tiled=True)  55.5 us
    reduce_scatter x1, waiting for transfers between devices, on_device(): lax.psum_scatter(fc2_term, 'dp', scatter_dimension=1, tiled=True)  55.1 us
    reduce_scatter x1, waiting for transfers between devices, on_device(): lax.psum_scatter(qkv_term, 'dp', scatter_dimension=1, tiled=True)  45 us
    unnamed x1, blocking collectives  39.2 us
    reduce_scatter x1, waiting for transfers between devices, on_device(): lax.psum_scatter(out_term, 'dp', scatter_dimension=1, tiled=True)  37.7 us
  transfers between devices with their start and end apart: 16, of which 14 were waited for; matrix products, arithmetic and copies ran while one was open for 5% of the time, Pallas kernels for 0%

commit v1 on v0

--- a/solution.py
+++ b/solution.py
@@ -1,6 +1,10 @@
+import functools
+
 import jax
 import jax.numpy as jnp
 from jax import lax
+from jax.experimental import pallas as pl
+from jax.experimental.pallas import tpu as pltpu
 from jax.sharding import PartitionSpec as P
 
 HEAD_DIM = 64
@@ -8,6 +12,232 @@
 
 EPSILON = 1e-06
 NEGATIVE = -1e30
+MESH = pl.DeviceIdType.MESH
+LANES = 128
+
+
+def peer_at(axis, k):
+    if axis == "all":
+        dp, tensor = lax.axis_size("dp"), lax.axis_size("tensor")
+        index = lax.rem(lax.axis_index("dp") * tensor + lax.axis_index("tensor") + k, dp * tensor)
+        return index, {"dp": index // tensor, "tensor": lax.rem(index, tensor)}
+    index = lax.rem(lax.axis_index(axis) + k, lax.axis_size(axis))
+    return index, {axis: index}
+
+
+def my_index(axis):
+    if axis == "all":
+        return lax.axis_index("dp") * lax.axis_size("tensor") + lax.axis_index("tensor")
+    return lax.axis_index(axis)
+
+
+def size_of(axis):
+    if axis == "all":
+        return lax.axis_size("dp") * lax.axis_size("tensor")
+    return lax.axis_size(axis)
+
+
+def view(ref, spot, index):
+    if spot is None:
+        return ref.at[index]
+    dim, width = spot
+    place = pl.ds(pl.multiple_of(index * width, width), width)
+    return ref.at[tuple([slice(None)] * dim + [place])]
+
+
+def for_each(count, body):
+    lax.fori_loop(0, count, lambda k, carry: (body(k), carry)[1], 0)
+
+
+class Gather:
+    def __init__(self, axis, block, spot=None):
+        self.axis, self.array, self.spot = axis, block, spot
+        shape = list(block.shape)
+        if spot is None:
+            shape = [size_of(axis)] + shape
+        else:
+            shape[spot[0]] *= size_of(axis)
+        self.out = jax.ShapeDtypeStruct(tuple(shape), block.dtype)
+        self.sems = [
+            pltpu.SemaphoreType.DMA((size_of(axis),)),
+            pltpu.SemaphoreType.DMA((size_of(axis),)),
+            pltpu.SemaphoreType.DMA,
+        ]
+
+    def own(self, src, out, sems):
+        return pltpu.make_async_copy(src, view(out, self.spot, my_index(self.axis)), sems[2])
+
+    def copy(self, src, out, sems, k):
+        _, device = peer_at(self.axis, k)
+        mine = view(out, self.spot, my_index(self.axis))
+        return pltpu.make_async_remote_copy(
+            src, mine, sems[0].at[k], sems[1].at[k], device_id=device, device_id_type=MESH
+        )
+
+    def start(self, src, out, sems):
+        for_each(size_of(self.axis) - 1, lambda k: self.copy(src, out, sems, k + 1).start())
+        self.own(src, out, sems).start()
+
+    def middle(self, src, out, sems):
+        pass
+
+    def finish(self, src, out, sems):
+        for_each(size_of(self.axis) - 1, lambda k: self.copy(src, out, sems, k + 1).wait())
+        self.own(src, out, sems).wait()
+
+
+class PairGather(Gather):
+    def __init__(self, block, spot=None):
+        super().__init__("dp", block, spot)
+        half = size_of("dp") // 2
+        self.sems = [pltpu.SemaphoreType.DMA((half,)) for _ in range(4)]
+        self.sems.append(pltpu.SemaphoreType.DMA)
+
+    def own(self, src, out, sems):
+        return pltpu.make_async_copy(src, view(out, self.spot, my_index("dp")), sems[4])
+
+    def away(self, src, out, sems, k):
+        _, device = peer_at("dp", 2 * k)
+        mine = view(out, self.spot, my_index("dp"))
+        return pltpu.make_async_remote_copy(
+            src, mine, sems[0].at[k], sems[1].at[k], device_id=device, device_id_type=MESH
+        )
+
+    def share(self, src, out, sems, k, first=False):
+        count = size_of("dp")
+        me = my_index("dp")
+        place = view(out, self.spot, lax.rem(me - 2 * k + count, count))
+        return pltpu.make_async_remote_copy(
+            src if first else place,
+            place,
+            sems[2].at[k],
+            sems[3].at[k],
+            device_id={"dp": me + 1 - 2 * lax.rem(me, 2)},
+            device_id_type=MESH,
+        )
+
+    def start(self, src, out, sems):
+        for_each(size_of("dp") // 2 - 1, lambda k: self.away(src, out, sems, k + 1).start())
+        self.share(src, out, sems, 0, True).start()
+        self.own(src, out, sems).start()
+
+    def middle(self, src, out, sems):
+        def pass_on(k):
+            self.away(src, out, sems, k + 1).wait_recv()
+            self.share(src, out, sems, k + 1).start()
+
+        for_each(size_of("dp") // 2 - 1, pass_on)
+
+    def finish(self, src, out, sems):
+        for_each(size_of("dp") // 2 - 1, lambda k: self.away(src, out, sems, k + 1).wait_send())
+        self.share(src, out, sems, 0, True).wait()
+        for_each(size_of("dp") // 2 - 1, lambda k: self.share(src, out, sems, k + 1).wait())
+        self.own(src, out, sems).wait()
+
+
+class Swap:
+    def __init__(self, axis, array, spot=None):
+        self.axis, self.array, self.spot = axis, array, spot
+        shape = list(array.shape)
+        if spot is None:
+            shape = shape[1:]
+        else:
+            shape[spot[0]] = spot[1]
+        self.out = jax.ShapeDtypeStruct((size_of(axis) - 1, *shape), array.dtype)
+        self.sems = [pltpu.SemaphoreType.DMA((size_of(axis),)) for _ in range(2)]
+
+    def copy(self, src, out, sems, k):
+        index, device = peer_at(self.axis, k)
+        return pltpu.make_async_remote_copy(
+            view(src, self.spot, index),
+            out.at[k - 1],
+            sems[0].at[k],
+            sems[1].at[k],
+            device_id=device,
+            device_id_type=MESH,
+        )
+
+    def start(self, src, out, sems):
+        for_each(size_of(self.axis) - 1, lambda k: self.copy(src, out, sems, k + 1).start())
+
+    def middle(self, src, out, sems):
+        pass
+
+    def finish(self, src, out, sems):
+        for_each(size_of(self.axis) - 1, lambda k: self.copy(src, out, sems, k + 1).wait())
+
+
+def exchange(number, *tasks):
+    axes = sorted({task.axis for task in tasks})
+    if "all" in axes:
+        axes = ["all"]
+    count = len(tasks)
+
+    def kernel(*refs):
+        sources, outs, sems = refs[:count], refs[count : 2 * count], list(refs[2 * count :])
+        grouped = []
+        for task in tasks:
+            grouped.append([sems.pop(0) for _ in task.sems])
+        barrier = pltpu.get_barrier_semaphore()
+
+        def greet(axis, k):
+            _, device = peer_at(axis, k)
+            pl.semaphore_signal(barrier, inc=1, device_id=device, device_id_type=MESH)
+
+        for axis in axes:
+            for_each(size_of(axis) - 1, functools.partial(lambda a, k: greet(a, k + 1), axis))
+        pl.semaphore_wait(barrier, sum(size_of(axis) - 1 for axis in axes))
+        for step in ("start", "middle", "finish"):
+            for task, src, out, own in zip(tasks, sources, outs, grouped):
+                getattr(task, step)(src, out, own)
+
+    return pl.pallas_call(
+        kernel,
+        out_shape=[task.out for task in tasks],
+        in_specs=[pl.BlockSpec(memory_space=pl.ANY)] * count,
+        out_specs=[pl.BlockSpec(memory_space=pl.ANY)] * count,
+        scratch_shapes=[sem for task in tasks for sem in task.sems],
+        compiler_params=pltpu.CompilerParams(collective_id=number, has_side_effects=True),
+    )(*[task.array for task in tasks])
+
+
+def spot_of(block, dim, width):
+    grain = LANES if dim == block.ndim - 1 else 16
+    return (dim, width) if width % grain == 0 else None
+
+
+def weight_gather(block, dim):
+    return PairGather(block, spot_of(block, dim, block.shape[dim]))
+
+
+def joined(gathered, block, dim):
+    if gathered.ndim == block.ndim:
+        return gathered
+    moved = jnp.moveaxis(gathered, 0, dim)
+    shape = list(block.shape)
+    shape[dim] *= gathered.shape[0]
+    return moved.reshape(shape)
+
+
+def grad_swap(term, dim):
+    count = size_of("dp")
+    width = term.shape[dim] // count
+    low = term.astype(jnp.bfloat16)
+    spot = spot_of(low, dim, width)
+    if spot is None:
+        shape = list(low.shape)
+        shape[dim : dim + 1] = [count, width]
+        low = jnp.moveaxis(low.reshape(shape), dim, 0)
+    return Swap("dp", low, spot)
+
+
+def own_part(term, axis, dim):
+    width = term.shape[dim] // size_of(axis)
+    return lax.dynamic_slice_in_dim(term, my_index(axis) * width, width, dim)
+
+
+def summed(own, others):
+    return own + jnp.sum(others.astype(jnp.float32), axis=0)
 
 
 def layer_norm(values, gain, shift):
@@ -53,41 +283,65 @@
     return (grad_query, grad_keys, grad_values)
 
 
+def row_validity(counts, seq, rows):
+    places = jnp.arange(rows, dtype=jnp.int32)
+    owner = places // seq
+    position = places - owner * seq
+    picks = owner[:, None] == jnp.arange(counts.shape[0], dtype=jnp.int32)[None, :]
+    return position < jnp.sum(jnp.where(picks, counts[None, :], 0), axis=1)
+
+
+def row_swap(part, rows):
+    return Swap("tensor", part.astype(jnp.bfloat16).reshape(-1, rows, part.shape[1]))
+
+
 def on_device(tokens, counts, vectors, fc1_bias, w_qkv, w_out, w_fc1, w_fc2, cotangent):
-    full_vectors, full_fc1 = (
-        lax.all_gather(vectors, ("dp", "tensor"), axis=1, tiled=True),
-        lax.all_gather(fc1_bias, ("dp", "tensor"), axis=0, tiled=True),
-    )
-    qkv_all, out_all, fc1_all, fc2_all = (
-        lax.all_gather(w_qkv, "dp", axis=1, tiled=True),
-        lax.all_gather(w_out, "dp", axis=1, tiled=True),
-        lax.all_gather(w_fc1, "dp", axis=0, tiled=True),
-        lax.all_gather(w_fc2, "dp", axis=1, tiled=True),
-    )
     tensor_count = lax.axis_size("tensor")
     tensor_index = lax.axis_index("tensor")
+    devices = size_of("all")
+    model_width = tokens.shape[1]
+    vector_size = vectors.size
+    small_size = vector_size + fc1_bias.size
+    small_rows = -(-small_size // (8 * LANES)) * 8
+    small = jnp.concatenate([vectors.reshape(-1), fc1_bias])
+    small = jnp.pad(small, (0, small_rows * LANES - small_size)).reshape(small_rows, LANES)
     local_rows = tokens.shape[0]
     block_rows = local_rows * tensor_count
     images = counts.shape[0]
+    local_valid = row_validity(counts, block_rows // images, block_rows)
+    local_valid = lax.dynamic_slice_in_dim(local_valid, tensor_index * local_rows, local_rows)
+    local_valid = local_valid.astype(jnp.float32)[:, None]
+    masked_out = local_valid * cotangent
+    small_all, gathered_grad, qkv_all, out_all = exchange(
+        0,
+        Gather("all", small),
+        Gather("tensor", masked_out.astype(jnp.bfloat16)),
+        weight_gather(w_qkv, 1),
+        weight_gather(w_out, 1),
+    )
+    qkv_all = joined(qkv_all, w_qkv, 1)
+    out_all = joined(out_all, w_out, 1)
+    gathered_grad = gathered_grad.reshape(block_rows, model_width)
+    small_all = small_all.reshape(devices, small_rows * LANES)
+    full_vectors = small_all[:, :vector_size].reshape(devices, vectors.shape[0], -1)
+    full_vectors = full_vectors.transpose(1, 0, 2).reshape(vectors.shape[0], model_width)
+    full_fc1 = small_all[:, vector_size:small_size].reshape(-1)
+    normed = layer_norm(tokens, full_vectors[0], full_vectors[1]).astype(jnp.bfloat16)
+    gathered, fc1_all, fc2_all = exchange(
+        1, Gather("tensor", normed), weight_gather(w_fc1, 0), weight_gather(w_fc2, 1)
+    )
+    gathered = gathered.reshape(block_rows, model_width)
+    fc1_all = joined(fc1_all, w_fc1, 0)
+    fc2_all = joined(fc2_all, w_fc2, 1)
     seq = block_rows // images
     width = qkv_all.shape[2]
-    model_width = qkv_all.shape[1]
     hidden_width = fc1_all.shape[1]
     heads_local = width // HEAD_DIM
     scale = HEAD_DIM ** (-0.5)
-    places = jnp.arange(block_rows, dtype=jnp.int32)
-    owner = places // seq
-    position = places - owner * seq
-    picks = owner[:, None] == jnp.arange(images, dtype=jnp.int32)[None, :]
-    row_count = jnp.sum(jnp.where(picks, counts[None, :], 0), axis=1)
-    block_valid = position < row_count
-    local_valid = lax.dynamic_slice_in_dim(block_valid, tensor_index * local_rows, local_rows)
-    local_valid = local_valid.astype(jnp.float32)[:, None]
+    block_valid = row_validity(counts, seq, block_rows)
     query_bias = lax.dynamic_slice_in_dim(full_vectors[2], tensor_index * width, width)
     value_bias = lax.dynamic_slice_in_dim(full_vectors[3], tensor_index * width, width)
     hidden_bias = lax.dynamic_slice_in_dim(full_fc1, tensor_index * hidden_width, hidden_width)
-    normed = layer_norm(tokens, full_vectors[0], full_vectors[1]).astype(jnp.bfloat16)
-    gathered = lax.all_gather(normed, "tensor", axis=0, tiled=True)
     projected = jnp.einsum("rd,kde->kre", gathered, qkv_all, preferred_element_type=jnp.float32)
     query = (
         (projected[0] + query_bias).astype(jnp.bfloat16).reshape(block_rows, heads_local, HEAD_DIM)
@@ -99,23 +353,17 @@
     mixed_one, total_one = attend(query, keys, values, block_valid, scale)
     mixed_all = mixed_one.reshape(block_rows, width).astype(jnp.bfloat16)
     attn_part = jnp.dot(mixed_all, out_all, preferred_element_type=jnp.float32)
-    attn_local = lax.psum_scatter(
-        attn_part.astype(jnp.bfloat16), "tensor", scatter_dimension=0, tiled=True
-    ).astype(jnp.float32)
+    (attn_others,) = exchange(2, row_swap(attn_part, local_rows))
+    attn_local = summed(own_part(attn_part, "tensor", 0), attn_others)
     middle = tokens + local_valid * (attn_local + full_vectors[4])
     normed2 = layer_norm(middle, full_vectors[5], full_vectors[6]).astype(jnp.bfloat16)
-    gathered2 = lax.all_gather(normed2, "tensor", axis=0, tiled=True)
+    (gathered2,) = exchange(3, Gather("tensor", normed2))
+    gathered2 = gathered2.reshape(block_rows, model_width)
     pre = jnp.dot(gathered2, fc1_all, preferred_element_type=jnp.float32) + hidden_bias
     hidden_float, gelu_back = jax.vjp(exact_gelu, pre)
     hidden = hidden_float.astype(jnp.bfloat16)
     mlp_part = jnp.dot(hidden, fc2_all, preferred_element_type=jnp.float32)
-    mlp_local = lax.psum_scatter(
-        mlp_part.astype(jnp.bfloat16), "tensor", scatter_dimension=0, tiled=True
-    ).astype(jnp.float32)
-    layer_out = middle + local_valid * (mlp_local + full_vectors[7])
-    masked_out = local_valid * cotangent
     grad_shift2 = jnp.sum(masked_out, axis=0)
-    gathered_grad = lax.all_gather(masked_out.astype(jnp.bfloat16), "tensor", axis=0, tiled=True)
     fc2_term = jnp.einsum("rf,rd->fd", hidden, gathered_grad, preferred_element_type=jnp.float32)
     grad_hidden = jnp.einsum(
         "rd,fd->rf", gathered_grad, fc2_all, preferred_element_type=jnp.float32
@@ -124,15 +372,25 @@
     hidden_bias_grad = jnp.sum(grad_pre.astype(jnp.float32), axis=0)
     fc1_term = jnp.einsum("rd,rf->df", gathered2, grad_pre, preferred_element_type=jnp.float32)
     normed2_part = jnp.einsum("rf,df->rd", grad_pre, fc1_all, preferred_element_type=jnp.float32)
-    grad_normed2 = lax.psum_scatter(
-        normed2_part.astype(jnp.bfloat16), "tensor", scatter_dimension=0, tiled=True
-    ).astype(jnp.float32)
+    normed2_others, mlp_others, fc1_others, fc2_others = exchange(
+        4,
+        row_swap(normed2_part, local_rows),
+        row_swap(mlp_part, local_rows),
+        grad_swap(fc1_term, 0),
+        grad_swap(fc2_term, 1),
+    )
+    grad_normed2 = summed(own_part(normed2_part, "tensor", 0), normed2_others)
+    mlp_local = summed(own_part(mlp_part, "tensor", 0), mlp_others)
+    layer_out = middle + local_valid * (mlp_local + full_vectors[7])
+    fc1_grad = summed(own_part(fc1_term, "dp", 0), fc1_others)
+    fc2_grad = summed(own_part(fc2_term, "dp", 1), fc2_others)
     second_norm, second_back = jax.vjp(layer_norm, middle, full_vectors[5], full_vectors[6])
     grad_through, gain2_grad, shift2_grad = second_back(grad_normed2)
     grad_middle = cotangent + grad_through
     masked_middle = local_valid * grad_middle
     out_bias_grad = jnp.sum(masked_middle, axis=0)
-    gathered_attn = lax.all_gather(masked_middle.astype(jnp.bfloat16), "tensor", axis=0, tiled=True)
+    (gathered_attn,) = exchange(5, Gather("tensor", masked_middle.astype(jnp.bfloat16)))
+    gathered_attn = gathered_attn.reshape(block_rows, model_width)
     out_term = jnp.einsum("re,rd->ed", mixed_all, gathered_attn, preferred_element_type=jnp.float32)
     grad_mixed = jnp.einsum("rd,ed->re", gathered_attn, out_all, preferred_element_type=jnp.float32)
     grad_mixed = grad_mixed.astype(jnp.bfloat16).reshape(block_rows, heads_local, HEAD_DIM)
@@ -147,15 +405,12 @@
     value_bias_grad = jnp.sum(grad_values.astype(jnp.float32), axis=0)
     qkv_term = jnp.einsum("rd,kre->kde", gathered, stacked, preferred_element_type=jnp.float32)
     normed_part = jnp.einsum("kre,kde->rd", stacked, qkv_all, preferred_element_type=jnp.float32)
-    qkv_grad, out_grad, fc1_grad, fc2_grad = (
-        lax.psum_scatter(qkv_term, "dp", scatter_dimension=1, tiled=True),
-        lax.psum_scatter(out_term, "dp", scatter_dimension=1, tiled=True),
-        lax.psum_scatter(fc1_term, "dp", scatter_dimension=0, tiled=True),
-        lax.psum_scatter(fc2_term, "dp", scatter_dimension=1, tiled=True),
-    )
-    grad_normed = lax.psum_scatter(
-        normed_part.astype(jnp.bfloat16), "tensor", scatter_dimension=0, tiled=True
-    ).astype(jnp.float32)
+    normed_others, qkv_others, out_others = exchange(
+        6, row_swap(normed_part, local_rows), grad_swap(qkv_term, 1), grad_swap(out_term, 1)
+    )
+    grad_normed = summed(own_part(normed_part, "tensor", 0), normed_others)
+    qkv_grad = summed(own_part(qkv_term, "dp", 1), qkv_others)
+    out_grad = summed(own_part(out_term, "dp", 1), out_others)
     first_norm, first_back = jax.vjp(layer_norm, tokens, full_vectors[0], full_vectors[1])
     grad_input_norm, gain1_grad, shift1_grad = first_back(grad_normed)
     input_grad = grad_middle + grad_input_norm
@@ -182,10 +437,16 @@
     hidden_bias_full = lax.dynamic_update_slice_in_dim(
         zeros_hidden, hidden_bias_grad, tensor_index * hidden_width, 0
     )
-    vectors_grad, fc1_bias_grad = (
-        lax.psum_scatter(vector_terms, ("dp", "tensor"), scatter_dimension=1, tiled=True),
-        lax.psum_scatter(hidden_bias_full, ("dp", "tensor"), scatter_dimension=0, tiled=True),
-    )
+    vector_blocks = vector_terms.reshape(vectors.shape[0], devices, -1).transpose(1, 0, 2)
+    small_terms = jnp.concatenate(
+        [vector_blocks.reshape(devices, -1), hidden_bias_full.reshape(devices, -1)], axis=1
+    )
+    small_terms = jnp.pad(small_terms, ((0, 0), (0, small_rows * LANES - small_size)))
+    small_terms = small_terms.reshape(devices, small_rows, LANES)
+    (small_others,) = exchange(7, Swap("all", small_terms))
+    small_grad = summed(own_part(small_terms, "all", 0)[0], small_others).reshape(-1)
+    vectors_grad = small_grad[:vector_size].reshape(vectors.shape)
+    fc1_bias_grad = small_grad[vector_size:small_size]
     return (
         layer_out,
         input_grad,

time: 804 us -> 367 us (0.46)
  waiting for transfers between devices: 501 us -> 0 us
  Pallas kernels: 0 us -> 256 us
  blocking collectives: 185 us -> 0 us
  between operations: 15.1 us -> 2.03 us
  other arithmetic: 25 us -> 36.3 us
    reduce_scatter x8 -> x0, waiting for transfers between devices: 302 us -> none  [the longest x1 55.5 us: on_device(): lax.psum_scatter(fc1_term, 'dp', scatter_dimension=0, tiled=True)]
    pallas_call x0 -> x8, Pallas kernels: none -> 256 us  [exchange(): pl.pallas_call(kernel, out_shape=[task.out for task in tasks], in_specs=[...]
    all_gather x3 -> x0, blocking collectives: 146 us -> none  [the longest x1 70.9 us: on_device(): lax.all_gather(vectors, ('dp', 'tensor'), axis=1, tiled=True)]
    all_gather x7 -> x0, waiting for transfers between devices: 124 us -> none  [the longest x1 33.8 us: on_device(): lax.all_gather(masked_out.astype(jnp.bfloat16), 'tensor', axis=0, tiled=T...]
    unnamed x17 -> x0, waiting for transfers between devices: 75 us -> none
    unnamed x1 -> x0, blocking collectives: 39.2 us -> none
    reduce_sum x0 -> x8, other arithmetic: none -> 8.09 us  [summed(): return own + jnp.sum(others.astype(jnp.float32), axis=0)]
  transfers between devices with their start and end apart: 16 -> 0, of which waited for: 14 -> 0; matrix products, arithmetic and copies ran while one was open for 5% -> 0% of each run, Pallas kernels for 0% -> 0%
where the time goes in v1:
time: 367 us; the launch traced here: 366 us
  Pallas kernels  256 us (70%)
  matrix products  56.3 us (15%)
  other arithmetic  36.3 us (10%)
  local copies, waits for them, and re-layouts  15.4 us (4%)
    pallas_call x8, Pallas kernels, exchange(): pl.pallas_call(kernel, out_shape=[task.out for task in tasks], in_specs=[...  256 us
    reduce_sum x8, other arithmetic, summed(): return own + jnp.sum(others.astype(jnp.float32), axis=0)  8.09 us
    dot_general x1, matrix products, on_device(): jnp.einsum('rd,fd->rf', gathered_grad, fc2_all, preferred_element_type=jn...  7.38 us

profile of v1, /device:TPU:0, one launch (start us, length us, event | category | flops | bytes accessed | tf_op | source)
XLA Modules:
  0.0 365.7 jit_solution(17647173678479157194)
XLA Ops:
  1.4 1.2 reduce_sum.245
  2.7 1.3 multiply_reduce_fusion.6
  4.0 0.8 reshape.270
  4.7 1.3 fusion.23.refs_0_
  6.0 1.9 multiply_convert_fusion.3.refs_1_
  7.9 32.9 %shard_map.152 = (f32[32,8,128]{2,1,0:T(8,128)}, bf16[4,152,1024]{2,1,0:T(8,128)(2,1)}, bf16[3,1024,256]{2,1,0:T(8,128)(2,1)}, bf16[256,1024]{1,0:T(8,128)(2,1)}) custom-call(f32[8,128]{1,0:T(8,128)} %fusion.23.refs_0_, bf16[152,1024]{1,0:T(8,128)(2,1)} %multiply_convert_fusion.3.refs_1_, bf16[3,128,256]{2,1,0:T(8,128)(2,1)} %refs_2_.2, bf16[256,128]{1,0:T(8,128)(2,1)} %refs_3_.1), custom_call_target="tpu_custom_call" | custom-call | tf_op jit(solution)/shard_map/pallas_call | solution.py:194
  40.8 1.0 copy.66
  43.2 0.9 add_convert_fusion.4.refs_0_
  44.1 35.8 %shard_map.153 = (bf16[4,152,1024]{2,1,0:T(8,128)(2,1)}, bf16[1024,1024]{1,0:T(8,128)(2,1)}, bf16[1024,1024]{1,0:T(8,128)(2,1)}) custom-call(bf16[152,1024]{1,0:T(8,128)(2,1)} %add_convert_fusion.4.refs_0_, bf16[128,1024]{1,0:T(8,128)(2,1)} %refs_1_.1, bf16[1024,128]{1,0:T(8,128)(2,1)} %refs_2_.3), custom_call_target="tpu_custom_call" | custom-call | tf_op jit(solution)/shard_map/pallas_call | solution.py:194
  80.0 2.4 convolution_bitcast_fusion.1
  83.2 1.6 fusion.34
  84.8 0.9 fusion
  85.7 1.7 copy-done
  87.5 1.2 fusion.17
  88.7 2.4 fusion.35
  91.1 24.7 %shard_map.154 = bf16[3,152,1024]{2,1,0:T(8,128)(2,1)} custom-call(bf16[4,152,1024]{2,1,0:T(8,128)(2,1)} %bitcast.92), custom_call_target="tpu_custom_call" | custom-call | tf_op jit(solution)/shard_map/pallas_call | solution.py:194
  115.8 1.4 convert_reduce_fusion.7
  117.2 1.3 fusion.32
  118.8 0.9 add_convert_fusion.3.refs_0_
  119.7 30.3 %shard_map.155 = bf16[4,152,1024]{2,1,0:T(8,128)(2,1)} custom-call(bf16[152,1024]{1,0:T(8,128)(2,1)} %add_convert_fusion.3.refs_0_), custom_call_target="tpu_custom_call" | custom-call | tf_op jit(solution)/shard_map/pallas_call | solution.py:194
  150.0 3.6 fusion.42
  153.6 7.4 %convert_reduce_fusion.3 = (f32[1024]{0:T(1024)S(1)}, bf16[608,1024]{1,0:T(8,128)(2,1)S(1)}, f32[608,1024]{1,0:T(8,128)S(1)}) fusion(f32[608,1024]{1,0:T(8,128)S(1)} %fusion.42, f32[1024]{0:T(1024)S(1)} %dynamic_slice.43, bf16[608,1024]{1,0:T(8,128)(2,1)S(1)} %bitcast.107, bf16[1024,1024]{1,0:T(8,128)(2,1)S(1)} %copy-done.21), kind=kOutput, calls=%fused_computation.16 | convolution fusion | flops 1321761792 | bytes 9576448 | tf_op jit(solution)/shard_map/rd,fd->rf/dot_general | solution.py:368
  161.0 0.6 multiply_convert_fusion.1
  161.6 0.5 dynamic_update_slice.13
  162.1 3.3 fusion.37
  165.4 3.4 fusion.36
  168.8 4.6 %fusion.38 = (bf16[1024,1024]{1,0:T(8,128)(2,1)}, f32[1024,1024]{1,0:T(8,128)}) fusion(bf16[608,1024]{1,0:T(8,128)(2,1)S(1)} %bitcast.86, bf16[608,1024]{1,0:T(8,128)(2,1)S(1)} %get-tuple-element.78), kind=kOutput, calls=%fused_computation.129 | convolution fusion | flops 1276116992 | bytes 8781824 | tf_op jit(solution)/shard_map/rd,rf->df/dot_general | solution.py:373
  173.4 4.6 %fusion.39 = (bf16[1024,1024]{1,0:T(8,128)(2,1)}, f32[1024,1024]{1,0:T(8,128)}) fusion(bf16[608,1024]{1,0:T(8,128)(2,1)S(1)} %multiply_convert_fusion.1, bf16[608,1024]{1,0:T(8,128)(2,1)S(1)} %bitcast.108), kind=kOutput, calls=%fused_computation.130 | convolution fusion | flops 1276116992 | bytes 8781824 | tf_op jit(solution)/shard_map/rf,rd->fd/dot_general | solution.py:367
  177.9 56.9 %shard_map.156 = (bf16[3,152,1024]{2,1,0:T(8,128)(2,1)}, bf16[3,152,1024]{2,1,0:T(8,128)(2,1)}, bf16[7,128,1024]{2,1,0:T(8,128)(2,1)}, bf16[7,1024,128]{2,1,0:T(8,128)(2,1)}) custom-call(bf16[4,152,1024]{2,1,0:T(8,128)(2,1)} %bitcast.105, bf16[4,152,1024]{2,1,0:T(8,128)(2,1)} %bitcast.104, bf16[1024,1024]{1,0:T(8,128)(2,1)} %get-tuple-element.99.refs_2_, ...), custom_call_target="tpu_custom_call" | custom-call | tf_op jit(solution)/shard_map/pallas_call | solution.py:194
  234.8 1.9 convert_reduce_fusion.5
  236.8 1.4 multiply_reduce_fusion.1
  238.2 2.3 fusion.31
  241.2 0.8 multiply_convert_fusion.2.refs_0_
  242.0 1.9 convert_reduce_fusion.1
  243.9 1.9 dynamic-slice_add_fusion.3
  246.1 1.9 dynamic-slice_add_fusion.2
  248.0 27.8 %shard_map.157 = bf16[4,152,1024]{2,1,0:T(8,128)(2,1)} custom-call(bf16[152,1024]{1,0:T(8,128)(2,1)} %multiply_convert_fusion.2.refs_0_), custom_call_target="tpu_custom_call" | custom-call | tf_op jit(solution)/shard_map/pallas_call | solution.py:194
  275.8 1.9 convolution_convert_fusion
  277.8 1.8 fusion.41
  279.8 4.0 %convert_reduce_fusion.9 = (f32[4,64]{1,0:T(4,128)S(1)}, bf16[4,64,608]{2,1,0:T(8,128)(2,1)S(1)}) fusion(bf16[608,4,64]{0,2,1:T(8,128)(2,1)S(1)} %bitcast.95, f32[4,608,608]{1,2,0:T(8,128)} %copy-done, f32[4,608]{1,0:T(4,128)S(1)} %log_add_fusion), kind=kOutput, calls=%fused_computation.50 | convolution fusion | flops 192691968 | bytes 6547968 | tf_op jit(solution)/shard_map/hqk,qhd->khd/dot_general | solution.py:274
  283.9 0.5 broadcast.243
  284.4 0.7 reduce.43
  285.1 0.9 copy.55
  286.1 4.7 %multiply_reduce_fusion = (f32[4,608]{1,0:T(4,128)S(1)}, f32[4,608,608]{1,2,0:T(8,128)S(1)}) fusion(f32[4,608,608]{1,2,0:T(8,128)} %copy-done, f32[4,608]{1,0:T(4,128)S(1)} %log_add_fusion, bf16[608,4,64]{0,2,1:T(8,128)(2,1)} %bitcast.96, f32[608,4,64]{0,2,1:T(8,128)} %bitcast.98, f32[4,64]{1,0:T(4,128)S(1)} %add.186), kind=kOutput, calls=%fused_computation.1 | convolution fusion | flops 194012800 | bytes 12783616 | tf_op jit(solution)/shard_map/qhd,khd->hqk/dot_general | solution.py:271
  290.9 1.5 multiply_convert_fusion
  292.4 1.1 fusion.13
  293.5 0.7 convert_reduce_fusion.10
  294.4 0.7 reduce.42
  295.5 4.5 %fusion.18 = f32[3,256,1024]{2,1,0:T(8,128)} fusion(bf16[608,1024,1]{1,0,2:T(8,128)(2,1)} %bitcast.118, bf16[1,608,256]{2,1,0:T(8,128)(2,1)S(1)} %copy-done.19, bf16[1,608,256]{2,1,0:T(8,128)(2,1)S(1)} %copy.54, bf16[1,608,256]{2,1,0:T(8,128)(2,1)S(1)} %copy.53), kind=kOutput, calls=%fused_computation.76 | convolution fusion | flops 957235200 | bytes 5324800 | tf_op jit(solution)/shard_map/rd,kre->kde/dot_general | solution.py:406
  300.0 3.2 fusion.40
  303.2 3.0 copy.56
  306.3 32.8 %shard_map.158 = (bf16[3,152,1024]{2,1,0:T(8,128)(2,1)}, bf16[7,3,128,256]{3,2,1,0:T(8,128)(2,1)}, bf16[7,256,128]{2,1,0:T(8,128)(2,1)}) custom-call(bf16[4,152,1024]{2,1,0:T(8,128)(2,1)} %bitcast.106, bf16[3,1024,256]{2,1,0:T(8,128)(2,1)} %bitcast.87, bf16[256,1024]{1,0:T(8,128)(2,1)} %get-tuple-element.107.refs_2_), custom_call_target="tpu_custom_call" | custom-call | tf_op jit(solution)/shard_map/pallas_call | solution.py:194
  339.0 1.4 convert_reduce_fusion.4
  340.5 1.5 multiply_reduce_fusion.2
  342.3 1.0 add_add_fusion.2
  343.7 0.7 copy.64
  344.4 14.5 %shard_map.159 = f32[31,8,128]{2,1,0:T(8,128)} custom-call(f32[32,8,128]{2,1,0:T(8,128)} %bitcast.109), custom_call_target="tpu_custom_call" | custom-call | tf_op jit(solution)/shard_map/pallas_call | solution.py:194
  358.9 0.9 reduce_sum.286
  359.9 0.7 bitcast_add_fusion.1
  360.6 0.5 slice_bitcast_fusion.1
  361.1 0.7 reshape.287
  361.8 1.6 dynamic-slice_add_fusion.4
  363.8 1.0 bitcast_add_fusion
  364.8 0.9 copy.58
  (114 shorter events, 5.7 us)
Async XLA Ops:
  0.6 42.6 %copy-start.1 = (f32[152,1024]{1,0:T(8,128)S(1)}, f32[152,1024]{1,0:T(8,128)}, u32[]{:S(2)}) copy-start(f32[152,1024]{1,0:T(8,128)} %param.9) | copy-start | bytes 1867780
  40.8 39.2 %copy-start.22 = (bf16[3,1024,256]{2,1,0:T(8,128)(2,1)S(1)}, bf16[3,1024,256]{2,1,0:T(8,128)(2,1)}, u32[]{:S(2)}) copy-start(bf16[3,1024,256]{2,1,0:T(8,128)(2,1)} %get-tuple-element.22) | copy-start | bytes 4718596
  82.7 2.1 copy-start.6
  83.0 2.7 copy-start.9
  84.8 2.6 copy-start
  87.5 1.3 copy-start.16
  88.7 2.4 copy-start.13
  150.0 3.6 copy-start.15
  150.0 3.6 copy-start.21
  162.1 3.3 copy-start.20
  165.4 3.4 copy-start.2
  238.2 2.4 copy-start.10
  240.8 5.3 %copy-start.3 = (f32[152,1024]{1,0:T(8,128)}, f32[152,1024]{1,0:T(8,128)S(1)}, u32[]{:S(2)}) copy-start(f32[152,1024]{1,0:T(8,128)S(1)} %get-tuple-element.76) | copy-start | bytes 1867780
  241.2 4.6 %copy-start.11 = (bf16[7,1024,128]{2,1,0:T(8,128)(2,1)S(1)}, bf16[7,1024,128]{2,1,0:T(8,128)(2,1)}, u32[]{:S(2)}) copy-start(bf16[7,1024,128]{2,1,0:T(8,128)(2,1)} %get-tuple-element.35) | copy-start | bytes 5505028
  245.8 30.0 %copy-start.17 = (bf16[256,1024]{1,0:T(8,128)(2,1)S(1)}, bf16[256,1024]{1,0:T(8,128)(2,1)}, u32[]{:S(2)}) copy-start(bf16[256,1024]{1,0:T(8,128)(2,1)} %get-tuple-element.25) | copy-start | bytes 1572868
  246.1 31.7 %copy-start.14 = (bf16[4,64,608]{2,1,0:T(8,128)(2,1)S(1)}, bf16[4,64,608]{2,1,0:T(8,128)(2,1)}, u32[]{:S(2)}) copy-start(bf16[4,64,608]{2,1,0:T(8,128)(2,1)} %copy-done.13) | copy-start | bytes 933892
  275.8 2.0 copy-start.5
  279.8 4.1 %copy-start.8 = (bf16[608,256]{0,1:T(8,128)(2,1)}, bf16[608,256]{0,1:T(8,128)(2,1)S(1)}, u32[]{:S(2)}) copy-start(bf16[608,256]{0,1:T(8,128)(2,1)S(1)} %copy.49) | copy-start | bytes 933892
  286.0 4.8 %slice-start = ((s8[6225920]{0:T(1024)(128)(4,1)}), s8[2031616]{0:T(1024)(128)(4,1)S(1)}, s32[]{:S(2)}) async-start(s8[6225920]{0:T(1024)(128)(4,1)} %bitcast.83), calls=%async_computation | async-start | bytes 4063232
  286.1 4.8 %slice-start.1 = ((s8[6225920]{0:T(1024)(128)(4,1)}), s8[4194304]{0:T(1024)(128)(4,1)S(1)}, s32[]{:S(2)}) async-start(s8[6225920]{0:T(1024)(128)(4,1)} %bitcast.83), calls=%async_computation.1 | async-start | bytes 8388608
  292.4 1.1 copy-start.7
  293.5 2.0 copy-start.19
  295.5 4.5 %copy-start.23 = (bf16[3,1024,256]{2,1,0:T(8,128)(2,1)S(1)}, bf16[3,1024,256]{2,1,0:T(8,128)(2,1)}, u32[]{:S(2)}) copy-start(bf16[3,1024,256]{2,1,0:T(8,128)(2,1)} %get-tuple-element.22) | copy-start | bytes 4718596
  340.4 1.8 copy-start.4
  341.9 19.8 %copy-start.18 = (bf16[7,256,128]{2,1,0:T(8,128)(2,1)S(1)}, bf16[7,256,128]{2,1,0:T(8,128)(2,1)}, u32[]{:S(2)}) copy-start(bf16[7,256,128]{2,1,0:T(8,128)(2,1)} %get-tuple-element.33) | copy-start | bytes 1376260
  342.3 21.1 %copy-start.12 = (bf16[7,3,128,256]{3,2,1,0:T(8,128)(2,1)S(1)}, bf16[7,3,128,256]{3,2,1,0:T(8,128)(2,1)}, u32[]{:S(2)}) copy-start(bf16[7,3,128,256]{3,2,1,0:T(8,128)(2,1)} %get-tuple-element.32) | copy-start | bytes 4128772

commit v2 on v1

--- a/solution.py
+++ b/solution.py
@@ -49,7 +49,14 @@
     lax.fori_loop(0, count, lambda k, carry: (body(k), carry)[1], 0)
 
 
-class Gather:
+class Task:
+    place = pl.ANY
+
+    def step(self, number, src, out, sems):
+        pass
+
+
+class Gather(Task):
     def __init__(self, axis, block, spot=None):
         self.axis, self.array, self.spot = axis, block, spot
         shape = list(block.shape)
@@ -78,9 +85,6 @@
         for_each(size_of(self.axis) - 1, lambda k: self.copy(src, out, sems, k + 1).start())
         self.own(src, out, sems).start()
 
-    def middle(self, src, out, sems):
-        pass
-
     def finish(self, src, out, sems):
         for_each(size_of(self.axis) - 1, lambda k: self.copy(src, out, sems, k + 1).wait())
         self.own(src, out, sems).wait()
@@ -121,7 +125,10 @@
         self.share(src, out, sems, 0, True).start()
         self.own(src, out, sems).start()
 
-    def middle(self, src, out, sems):
+    def step(self, number, src, out, sems):
+        if number != 2:
+            return
+
         def pass_on(k):
             self.away(src, out, sems, k + 1).wait_recv()
             self.share(src, out, sems, k + 1).start()
@@ -135,7 +142,7 @@
         self.own(src, out, sems).wait()
 
 
-class Swap:
+class Swap(Task):
     def __init__(self, axis, array, spot=None):
         self.axis, self.array, self.spot = axis, array, spot
         shape = list(array.shape)
@@ -160,11 +167,142 @@
     def start(self, src, out, sems):
         for_each(size_of(self.axis) - 1, lambda k: self.copy(src, out, sems, k + 1).start())
 
-    def middle(self, src, out, sems):
-        pass
-
     def finish(self, src, out, sems):
         for_each(size_of(self.axis) - 1, lambda k: self.copy(src, out, sems, k + 1).wait())
+
+
+class Line(Task):
+    axis = "tensor"
+
+    def remote(self, src, dst, sems, way, index):
+        target = lax.axis_index("tensor") + (1 - 2 * way)
+        return pltpu.make_async_remote_copy(
+            src,
+            dst,
+            sems[0].at[way, index],
+            sems[1].at[way, index],
+            device_id={"tensor": target},
+            device_id_type=MESH,
+        )
+
+
+class LineGather(Line):
+    def __init__(self, block):
+        self.array = block
+        count = size_of("tensor")
+        self.out = jax.ShapeDtypeStruct((count, *block.shape), block.dtype)
+        self.sems = [
+            pltpu.SemaphoreType.DMA((2, count)),
+            pltpu.SemaphoreType.DMA((2, count)),
+            pltpu.SemaphoreType.DMA,
+        ]
+
+    def own(self, src, out, sems):
+        return pltpu.make_async_copy(src, out.at[lax.axis_index("tensor")], sems[2])
+
+    def start(self, src, out, sems):
+        me, last = lax.axis_index("tensor"), size_of("tensor") - 1
+        pl.when(me < last)(lambda: self.remote(src, out.at[me], sems, 0, me).start())
+        pl.when(me > 0)(lambda: self.remote(src, out.at[me], sems, 1, me).start())
+        self.own(src, out, sems).start()
+
+    def step(self, number, src, out, sems):
+        me, last = lax.axis_index("tensor"), size_of("tensor") - 1
+        for way, index, here, more in (
+            (0, me - number, me >= number, me < last),
+            (1, me + number, me + number <= last, me > 0),
+        ):
+
+            @pl.when(here)
+            def _():
+                copy = self.remote(out.at[index], out.at[index], sems, way, index)
+                copy.wait_recv()
+                pl.when(more)(copy.start)
+
+    def finish(self, src, out, sems):
+        me, last = lax.axis_index("tensor"), size_of("tensor") - 1
+        for number in range(last + 1):
+            for way, index, sent in (
+                (0, me - number, (me >= number) & (me < last)),
+                (1, me + number, (me + number <= last) & (me > 0)),
+            ):
+                copy = self.remote(src, out.at[me], sems, way, index)
+                pl.when(sent)(copy.wait_send)
+        self.own(src, out, sems).wait()
+
+
+class LineSum(Line):
+    place = pltpu.VMEM
+
+    def __init__(self, blocks):
+        self.array = blocks
+        count = blocks.shape[0]
+        self.out = jax.ShapeDtypeStruct((2, *blocks.shape[1:]), blocks.dtype)
+        self.sems = [
+            pltpu.SemaphoreType.DMA((2, count)),
+            pltpu.SemaphoreType.DMA((2, count)),
+            pltpu.VMEM((2, *blocks.shape), blocks.dtype),
+        ]
+
+    def start(self, src, out, sems):
+        self.move(0, src, sems)
+
+    def step(self, number, src, out, sems):
+        if number < size_of("tensor") - 1:
+            self.move(number, src, sems)
+
+    def routes(self, number):
+        me, last = lax.axis_index("tensor"), size_of("tensor") - 1
+        up, down = number - me, number - (last - me)
+        return (
+            (0, last - up, (up >= 0) & (last - up > me), me > 0),
+            (1, down, (down >= 0) & (down < me), me < last),
+        )
+
+    def move(self, number, src, sems):
+        held = sems[2]
+        for way, index, sends, follows in self.routes(number):
+
+            @pl.when(sends)
+            def _():
+                slot = held.at[way, index]
+
+                @pl.when(follows)
+                def _():
+                    self.remote(slot, slot, sems, way, index).wait_recv()
+                    self.add(src, held, way, index)
+                    self.remote(slot, slot, sems, way, index).start()
+
+                @pl.when(jnp.logical_not(follows))
+                def _():
+                    self.remote(src.at[index], slot, sems, way, index).start()
+
+    def add(self, src, held, way, index):
+        width = 2 * LANES
+        for at in range(0, held.shape[3], width):
+            part = held[way, index, :, at : at + width].astype(jnp.float32)
+            part += src[index, :, at : at + width].astype(jnp.float32)
+            held[way, index, :, at : at + width] = part.astype(held.dtype)
+
+    def finish(self, src, out, sems):
+        me, last = lax.axis_index("tensor"), size_of("tensor") - 1
+        held = sems[2]
+        for way, comes in ((0, me > 0), (1, me < last)):
+
+            @pl.when(comes)
+            def _():
+                slot = held.at[way, me]
+                self.remote(slot, slot, sems, way, me).wait_recv()
+                out[way] = held[way, me]
+
+            @pl.when(jnp.logical_not(comes))
+            def _():
+                out[way] = jnp.zeros(out.shape[1:], out.dtype)
+
+        for number in range(last):
+            for way, index, sends, _ in self.routes(number):
+                slot = held.at[way, index]
+                pl.when(sends)(self.remote(slot, slot, sems, way, index).wait_send)
 
 
 def exchange(number, *tasks):
@@ -187,17 +325,24 @@
         for axis in axes:
             for_each(size_of(axis) - 1, functools.partial(lambda a, k: greet(a, k + 1), axis))
         pl.semaphore_wait(barrier, sum(size_of(axis) - 1 for axis in axes))
-        for step in ("start", "middle", "finish"):
-            for task, src, out, own in zip(tasks, sources, outs, grouped):
-                getattr(task, step)(src, out, own)
+        every = list(zip(tasks, sources, outs, grouped))
+        for task, src, out, own in every:
+            task.start(src, out, own)
+        for step in range(1, size_of("tensor")):
+            for task, src, out, own in every:
+                task.step(step, src, out, own)
+        for task, src, out, own in every:
+            task.finish(src, out, own)
 
     return pl.pallas_call(
         kernel,
         out_shape=[task.out for task in tasks],
-        in_specs=[pl.BlockSpec(memory_space=pl.ANY)] * count,
-        out_specs=[pl.BlockSpec(memory_space=pl.ANY)] * count,
+        in_specs=[pl.BlockSpec(memory_space=task.place) for task in tasks],
+        out_specs=[pl.BlockSpec(memory_space=task.place) for task in tasks],
         scratch_shapes=[sem for task in tasks for sem in task.sems],
-        compiler_params=pltpu.CompilerParams(collective_id=number, has_side_effects=True),
+        compiler_params=pltpu.CompilerParams(
+            collective_id=number, has_side_effects=True, vmem_limit_bytes=24 * 2**20
+        ),
     )(*[task.array for task in tasks])
 
 
@@ -291,8 +436,20 @@
     return position < jnp.sum(jnp.where(picks, counts[None, :], 0), axis=1)
 
 
-def row_swap(part, rows):
-    return Swap("tensor", part.astype(jnp.bfloat16).reshape(-1, rows, part.shape[1]))
+def row_sum(part, rows):
+    return LineSum(part.astype(jnp.bfloat16).reshape(-1, rows, part.shape[1]))
+
+
+def row_permutes(part, rows):
+    count = size_of("tensor")
+    parts = part.reshape(count, rows, part.shape[1])
+    others = []
+    for k in range(1, count):
+        index, _ = peer_at("tensor", k)
+        block = lax.dynamic_index_in_dim(parts, index, 0, keepdims=False)
+        pairs = [(i, (i + k) % count) for i in range(count)]
+        others.append(lax.ppermute(block, "tensor", pairs))
+    return others
 
 
 def on_device(tokens, counts, vectors, fc1_bias, w_qkv, w_out, w_fc1, w_fc2, cotangent):
@@ -315,7 +472,7 @@
     small_all, gathered_grad, qkv_all, out_all = exchange(
         0,
         Gather("all", small),
-        Gather("tensor", masked_out.astype(jnp.bfloat16)),
+        LineGather(masked_out.astype(jnp.bfloat16)),
         weight_gather(w_qkv, 1),
         weight_gather(w_out, 1),
     )
@@ -327,15 +484,11 @@
     full_vectors = full_vectors.transpose(1, 0, 2).reshape(vectors.shape[0], model_width)
     full_fc1 = small_all[:, vector_size:small_size].reshape(-1)
     normed = layer_norm(tokens, full_vectors[0], full_vectors[1]).astype(jnp.bfloat16)
-    gathered, fc1_all, fc2_all = exchange(
-        1, Gather("tensor", normed), weight_gather(w_fc1, 0), weight_gather(w_fc2, 1)
-    )
+    (gathered,) = exchange(1, LineGather(normed))
     gathered = gathered.reshape(block_rows, model_width)
-    fc1_all = joined(fc1_all, w_fc1, 0)
-    fc2_all = joined(fc2_all, w_fc2, 1)
     seq = block_rows // images
     width = qkv_all.shape[2]
-    hidden_width = fc1_all.shape[1]
+    hidden_width = w_fc1.shape[1]
     heads_local = width // HEAD_DIM
     scale = HEAD_DIM ** (-0.5)
     block_valid = row_validity(counts, seq, block_rows)
@@ -353,11 +506,13 @@
     mixed_one, total_one = attend(query, keys, values, block_valid, scale)
     mixed_all = mixed_one.reshape(block_rows, width).astype(jnp.bfloat16)
     attn_part = jnp.dot(mixed_all, out_all, preferred_element_type=jnp.float32)
-    (attn_others,) = exchange(2, row_swap(attn_part, local_rows))
+    attn_others, fc1_all = exchange(2, row_sum(attn_part, local_rows), weight_gather(w_fc1, 0))
+    fc1_all = joined(fc1_all, w_fc1, 0)
     attn_local = summed(own_part(attn_part, "tensor", 0), attn_others)
     middle = tokens + local_valid * (attn_local + full_vectors[4])
     normed2 = layer_norm(middle, full_vectors[5], full_vectors[6]).astype(jnp.bfloat16)
-    (gathered2,) = exchange(3, Gather("tensor", normed2))
+    gathered2, fc2_all = exchange(3, LineGather(normed2), weight_gather(w_fc2, 1))
+    fc2_all = joined(fc2_all, w_fc2, 1)
     gathered2 = gathered2.reshape(block_rows, model_width)
     pre = jnp.dot(gathered2, fc1_all, preferred_element_type=jnp.float32) + hidden_bias
     hidden_float, gelu_back = jax.vjp(exact_gelu, pre)
@@ -372,24 +527,28 @@
     hidden_bias_grad = jnp.sum(grad_pre.astype(jnp.float32), axis=0)
     fc1_term = jnp.einsum("rd,rf->df", gathered2, grad_pre, preferred_element_type=jnp.float32)
     normed2_part = jnp.einsum("rf,df->rd", grad_pre, fc1_all, preferred_element_type=jnp.float32)
-    normed2_others, mlp_others, fc1_others, fc2_others = exchange(
-        4,
-        row_swap(normed2_part, local_rows),
-        row_swap(mlp_part, local_rows),
-        grad_swap(fc1_term, 0),
-        grad_swap(fc2_term, 1),
+    normed2_others, fc2_others = exchange(
+        4, row_sum(normed2_part, local_rows), grad_swap(fc2_term, 1)
     )
     grad_normed2 = summed(own_part(normed2_part, "tensor", 0), normed2_others)
-    mlp_local = summed(own_part(mlp_part, "tensor", 0), mlp_others)
-    layer_out = middle + local_valid * (mlp_local + full_vectors[7])
-    fc1_grad = summed(own_part(fc1_term, "dp", 0), fc1_others)
     fc2_grad = summed(own_part(fc2_term, "dp", 1), fc2_others)
     second_norm, second_back = jax.vjp(layer_norm, middle, full_vectors[5], full_vectors[6])
     grad_through, gain2_grad, shift2_grad = second_back(grad_normed2)
     grad_middle = cotangent + grad_through
     masked_middle = local_valid * grad_middle
     out_bias_grad = jnp.sum(masked_middle, axis=0)
-    (gathered_attn,) = exchange(5, Gather("tensor", masked_middle.astype(jnp.bfloat16)))
+    gathered_attn, fc1_others = exchange(
+        5, LineGather(masked_middle.astype(jnp.bfloat16)), grad_swap(fc1_term, 0)
+    )
+    fc1_grad = summed(own_part(fc1_term, "dp", 0), fc1_others)
+    gathered_attn, mlp_low = lax.optimization_barrier(
+        (gathered_attn, mlp_part.astype(jnp.bfloat16))
+    )
+    mlp_others = row_permutes(mlp_low, local_rows)
+    mlp_local = own_part(mlp_part, "tensor", 0)
+    for block in mlp_others:
+        mlp_local = mlp_local + block.astype(jnp.float32)
+    layer_out = middle + local_valid * (mlp_local + full_vectors[7])
     gathered_attn = gathered_attn.reshape(block_rows, model_width)
     out_term = jnp.einsum("re,rd->ed", mixed_all, gathered_attn, preferred_element_type=jnp.float32)
     grad_mixed = jnp.einsum("rd,ed->re", gathered_attn, out_all, preferred_element_type=jnp.float32)
@@ -406,7 +565,7 @@
     qkv_term = jnp.einsum("rd,kre->kde", gathered, stacked, preferred_element_type=jnp.float32)
     normed_part = jnp.einsum("kre,kde->rd", stacked, qkv_all, preferred_element_type=jnp.float32)
     normed_others, qkv_others, out_others = exchange(
-        6, row_swap(normed_part, local_rows), grad_swap(qkv_term, 1), grad_swap(out_term, 1)
+        6, row_sum(normed_part, local_rows), grad_swap(qkv_term, 1), grad_swap(out_term, 1)
     )
     grad_normed = summed(own_part(normed_part, "tensor", 0), normed_others)
     qkv_grad = summed(own_part(qkv_term, "dp", 1), qkv_others)

time: 367 us -> 316 us (0.86)
  Pallas kernels: 256 us -> 199 us
  local copies, waits for them, and re-layouts: 15.4 us -> 31.2 us
  other arithmetic: 36.3 us -> 26.2 us
  starting transfers between devices: 0 us -> 3.83 us
    pallas_call x8, Pallas kernels: 256 us -> 199 us  [exchange(): pl.pallas_call(kernel, out_shape=[task.out for task in tasks], in_specs=[...]
    unnamed x55 -> x91, local copies, waits for them, and re-layouts: 4.57 us -> 11.6 us
    reduce_sum x8, other arithmetic: 8.09 us -> 2.76 us  [summed(): return own + jnp.sum(others.astype(jnp.float32), axis=0)]
    ppermute x0 -> x3, starting transfers between devices: none -> 3.83 us  [row_permutes(): others.append(lax.ppermute(block, 'tensor', pairs))]
  transfers between devices with their start and end apart: 0 -> 3, of which waited for: 0 -> 0; matrix products, arithmetic and copies ran while one was open for 0% -> 15% of each run, Pallas kernels for 0% -> 8%
where the time goes in v2:
time: 316 us; the launch traced here: 315 us
  Pallas kernels  199 us (63%)
  matrix products  52.7 us (17%)
  local copies, waits for them, and re-layouts  31.2 us (10%)
  other arithmetic  26.2 us (8%)
  starting transfers between devices  3.83 us (1%)
    pallas_call x8, Pallas kernels, exchange(): pl.pallas_call(kernel, out_shape=[task.out for task in tasks], in_specs=[...  199 us
    unnamed x91, local copies, waits for them, and re-layouts  11.6 us
    dot_general x1, matrix products, on_device(): jnp.einsum('rd,fd->rf', gathered_grad, fc2_all, preferred_element_type=jn...  7.39 us
    add x5, other arithmetic, summed(): return own + jnp.sum(others.astype(jnp.float32), axis=0)  7.25 us
  transfers between devices with their start and end apart: 3, of which 0 were waited for; matrix products, arithmetic and copies ran while one was open for 15% of the time, Pallas kernels for 8%

profile of v2, /device:TPU:0, one launch (start us, length us, event | category | flops | bytes accessed | tf_op | source)
XLA Modules:
  0.0 314.5 jit_solution(4265330690965974792)
XLA Ops:
  1.3 0.8 reshape.270
  2.2 0.7 fusion.23.refs_0_
  2.8 1.2 multiply_convert_fusion.3.refs_1_
  4.0 0.9 copy-done.7
  5.0 0.8 copy-done.8
  5.8 35.1 %shard_map.152 = (f32[32,8,128]{2,1,0:T(8,128)S(1)}, bf16[4,152,1024]{2,1,0:T(8,128)(2,1)S(1)}, bf16[3,1024,256]{2,1,0:T(8,128)(2,1)S(1)}, bf16[256,1024]{1,0:T(8,128)(2,1)S(1)}) custom-call(f32[8,128]{1,0:T(8,128)S(1)} %fusion.23.refs_0_, bf16[152,1024]{1,0:T(8,128)(2,1)S(1)} %multiply_convert_fusion.3.refs_1_, bf16[3,128,256]{2,1,0:T(8,128)(2,1)S(1)} %copy-done.7, ...), custom_call_target="tpu_custom_call" | custom-call | tf_op jit(solution)/shard_map/pallas_call | solution.py:337
  41.0 0.7 slice_bitcast_fusion
  41.7 1.2 reduce_sum.237
  42.9 1.3 multiply_reduce_fusion.6
  45.4 1.0 slice_reduce_fusion
  46.3 0.8 mul.235
  47.1 0.8 add.207
  47.9 1.3 add_convert_fusion.4.refs_0_
  49.2 21.4 %shard_map.153 = bf16[4,152,1024]{2,1,0:T(8,128)(2,1)S(1)} custom-call(bf16[152,1024]{1,0:T(8,128)(2,1)S(1)} %add_convert_fusion.4.refs_0_), custom_call_target="tpu_custom_call" | custom-call | tf_op jit(solution)/shard_map/pallas_call | solution.py:337
  70.6 1.1 convolution_bitcast_fusion.1
  71.8 0.8 slice.100
  72.6 0.9 fusion.33
  74.6 1.5 copy.46
  76.2 1.6 fusion.34
  77.8 0.9 fusion
  78.7 1.7 copy-done.13
  80.4 1.2 fusion.17
  82.7 24.7 %shard_map.154 = (bf16[2,152,1024]{2,1,0:T(8,128)(2,1)S(1)}, bf16[1024,1024]{1,0:T(8,128)(2,1)S(1)}) custom-call(bf16[4,152,1024]{2,1,0:T(8,128)(2,1)S(1)} %bitcast.90, bf16[128,1024]{1,0:T(8,128)(2,1)S(1)} %copy-done.6), custom_call_target="tpu_custom_call" | custom-call | tf_op jit(solution)/shard_map/pallas_call | solution.py:337
  107.5 1.3 copy-done.9
  109.4 0.7 dynamic_slice.53
  110.3 27.7 %shard_map.155 = (bf16[4,152,1024]{2,1,0:T(8,128)(2,1)S(1)}, bf16[1024,1024]{1,0:T(8,128)(2,1)S(1)}) custom-call(bf16[152,1024]{1,0:T(8,128)(2,1)S(1)} %add_convert_fusion.3.refs_0_, bf16[1024,128]{1,0:T(8,128)(2,1)S(1)} %copy-done.5), custom_call_target="tpu_custom_call" | custom-call | tf_op jit(solution)/shard_map/pallas_call | solution.py:337
  138.1 3.1 fusion.42
  141.1 7.4 %convert_reduce_fusion.3 = (f32[1024]{0:T(1024)S(1)}, bf16[608,1024]{1,0:T(8,128)(2,1)S(1)}, f32[608,1024]{1,0:T(8,128)S(1)}) fusion(f32[608,1024]{1,0:T(8,128)S(1)} %fusion.42, f32[1024]{0:T(1024)S(1)} %dynamic_slice.53, bf16[608,1024]{1,0:T(8,128)(2,1)S(1)} %bitcast.99, bf16[1024,1024]{1,0:T(8,128)(2,1)S(1)} %get-tuple-element.31), kind=kOutput, calls=%fused_computation.16 | convolution fusion | flops 1321761792 | bytes 9576448 | tf_op jit(solution)/shard_map/rd,fd->rf/dot_general | solution.py:523
  148.5 1.5 fusion.36
  150.0 3.9 %fusion.38 = (bf16[1024,1024]{1,0:T(8,128)(2,1)S(1)}, f32[1024,1024]{1,0:T(8,128)}) fusion(bf16[608,1024]{1,0:T(8,128)(2,1)S(1)} %bitcast.92, bf16[608,1024]{1,0:T(8,128)(2,1)S(1)} %get-tuple-element.84), kind=kOutput, calls=%fused_computation.131 | convolution fusion | flops 1276116992 | bytes 8781824 | tf_op jit(solution)/shard_map/rd,rf->df/dot_general | solution.py:528
  154.5 3.3 %fusion.39 = (bf16[608,1024]{1,0:T(8,128)(2,1)}, f32[608,1024]{1,0:T(8,128)}) fusion(bf16[608,1024]{1,0:T(8,128)(2,1)S(1)} %multiply_convert_fusion.1, bf16[1024,1024]{1,0:T(8,128)(2,1)S(1)} %get-tuple-element.31), kind=kOutput, calls=%fused_computation.132 | convolution fusion | flops 1275691008 | bytes 7077888 | tf_op jit(solution)/shard_map/dot_general | solution.py:520
  157.9 3.9 %fusion.37 = (bf16[1024,1024]{1,0:T(8,128)(2,1)S(1)}, f32[1024,1024]{1,0:T(8,128)}) fusion(bf16[608,1024]{1,0:T(8,128)(2,1)S(1)} %multiply_convert_fusion.1, bf16[608,1024]{1,0:T(8,128)(2,1)S(1)} %bitcast.100), kind=kOutput, calls=%fused_computation.130 | convolution fusion | flops 1276116992 | bytes 8781824 | tf_op jit(solution)/shard_map/rf,rd->fd/dot_general | solution.py:522
  161.8 24.7 %shard_map.156 = (bf16[2,152,1024]{2,1,0:T(8,128)(2,1)S(1)}, bf16[7,1024,128]{2,1,0:T(8,128)(2,1)S(1)}) custom-call(bf16[4,152,1024]{2,1,0:T(8,128)(2,1)S(1)} %bitcast.98, bf16[1024,1024]{1,0:T(8,128)(2,1)S(1)} %get-tuple-element.105.refs_1_), custom_call_target="tpu_custom_call" | custom-call | tf_op jit(solution)/shard_map/pallas_call | solution.py:337
  188.0 0.8 copy-done.20
  188.8 27.8 %shard_map.157 = (bf16[4,152,1024]{2,1,0:T(8,128)(2,1)S(1)}, bf16[7,128,1024]{2,1,0:T(8,128)(2,1)S(1)}) custom-call(bf16[152,1024]{1,0:T(8,128)(2,1)S(1)} %multiply_convert_fusion.2.refs_0_, bf16[1024,1024]{1,0:T(8,128)(2,1)S(1)} %get-tuple-element.107.refs_1_), custom_call_target="tpu_custom_call" | custom-call | tf_op jit(solution)/shard_map/pallas_call | solution.py:337
  216.6 1.2 copy-done
  217.8 2.6 dynamic-slice_bitcast_fusion.2
  220.4 3.8 %collective-permute-start.2 = (bf16[152,1024]{1,0:T(8,128)(2,1)}, bf16[152,1024]{1,0:T(8,128)(2,1)}, u32[]{:S(2)}, u32[]{:S(2)}) collective-permute-start(bf16[152,1024]{1,0:T(8,128)(2,1)} %get-tuple-element.97), channel_id=1, source_target_pairs={{0,3},{1,0},{2,1},{3,2},{4,7},{5,4},{6,5},{7,6},{8,11},{9,8},{10,9... | collective-permute-start | bytes 933896 | tf_op jit(solution)/shard_map/ppermute | solution.py:451
  224.2 2.3 convolution_convert_fusion
  226.6 2.9 fusion.41
  229.7 4.7 %convert_reduce_fusion.8 = (f32[4,64]{1,0:T(4,128)S(1)}, bf16[4,64,608]{2,1,0:T(8,128)(2,1)}) fusion(bf16[608,4,64]{0,2,1:T(8,128)(2,1)S(1)} %bitcast.110, f32[4,608,608]{1,2,0:T(8,128)} %copy-done.13, f32[4,608]{1,0:T(4,128)S(1)} %log_add_fusion), kind=kOutput, calls=%fused_computation.49 | convolution fusion | flops 192691968 | bytes 6547968 | tf_op jit(solution)/shard_map/hqk,qhd->khd/dot_general | solution.py:419
  234.4 4.4 %multiply_reduce_fusion = (f32[4,608]{1,0:T(4,128)S(1)}, f32[4,608,608]{1,2,0:T(8,128)S(1)}) fusion(f32[4,608,608]{1,2,0:T(8,128)} %copy-done.13, f32[4,608]{1,0:T(4,128)S(1)} %log_add_fusion, bf16[608,4,64]{0,2,1:T(8,128)(2,1)S(1)} %bitcast.111, f32[608,4,64]{0,2,1:T(8,128)S(1)} %bitcast.113, f32[4,64]{1,0:T(4,128)S(1)} %add.211), kind=kOutput, calls=%fused_computation.1 | convolution fusion | flops 194012800 | bytes 12783616 | tf_op jit(solution)/shard_map/qhd,khd->hqk/dot_general | solution.py:416
  238.9 1.3 multiply_convert_fusion
  240.2 1.8 fusion.13
  242.0 1.4 convert_reduce_fusion.9
  243.5 1.1 copy.53
  244.7 0.9 copy.54
  245.6 4.6 %fusion.18 = f32[3,256,1024]{2,1,0:T(8,128)} fusion(bf16[608,1024,1]{1,0,2:T(8,128)(2,1)} %bitcast.94, bf16[1,608,256]{2,1,0:T(8,128)(2,1)S(1)} %copy.55, bf16[1,608,256]{2,1,0:T(8,128)(2,1)} %copy.54, bf16[1,608,256]{2,1,0:T(8,128)(2,1)S(1)} %copy.53), kind=kOutput, calls=%fused_computation.75 | convolution fusion | flops 957235200 | bytes 5324800 | tf_op jit(solution)/shard_map/rd,kre->kde/dot_general | solution.py:565
  250.2 3.0 fusion.40
  254.5 0.7 reduce.43
  255.3 1.9 convert_reduce_fusion.1
  257.2 2.2 copy.56
  259.4 1.3 copy-done.3
  260.7 26.4 %shard_map.158 = (bf16[2,152,1024]{2,1,0:T(8,128)(2,1)S(1)}, bf16[7,3,128,256]{3,2,1,0:T(8,128)(2,1)S(1)}, bf16[7,256,128]{2,1,0:T(8,128)(2,1)S(1)}) custom-call(bf16[4,152,1024]{2,1,0:T(8,128)(2,1)S(1)} %bitcast.97, bf16[3,1024,256]{2,1,0:T(8,128)(2,1)S(1)} %bitcast.89, bf16[256,1024]{1,0:T(8,128)(2,1)S(1)} %get-tuple-element.115.refs_2_), custom_call_target="tpu_custom_call" | custom-call | tf_op jit(solution)/shard_map/pallas_call | solution.py:337
  287.6 1.8 bitcast_add_fusion
  289.4 2.0 dynamic-slice_add_fusion.2
  291.4 1.6 dynamic-slice_add_fusion.4
  293.0 0.7 reduce.42
  293.8 1.9 copy.58
  295.8 1.9 dynamic-slice_add_fusion.3
  297.8 2.9 multiply_reduce_fusion.2
  301.2 10.8 %shard_map.159 = f32[31,8,128]{2,1,0:T(8,128)S(1)} custom-call(f32[32,8,128]{2,1,0:T(8,128)S(1)} %bitcast.101), custom_call_target="tpu_custom_call" | custom-call | tf_op jit(solution)/shard_map/pallas_call | solution.py:337
  312.9 0.7 reshape.287
  313.6 1.0 add_add_fusion.2
  (157 shorter events, 10.5 us)
Async XLA Ops:
  1.3 1.5 copy-start.40
  2.2 38.8 %copy-start.33 = (f32[152]{0:T(256)}, f32[152]{0:T(256)S(1)}, u32[]{:S(2)}) copy-start(f32[152]{0:T(256)S(1)} %dynamic-slice_convert_fusion) | copy-start | bytes 1828
  4.0 0.9 copy-start.7
  5.0 0.8 copy-start.8
  40.9 30.9 %copy-start.11 = (bf16[3,1024,256]{2,1,0:T(8,128)(2,1)}, bf16[3,1024,256]{2,1,0:T(8,128)(2,1)S(1)}, u32[]{:S(2)}) copy-start(bf16[3,1024,256]{2,1,0:T(8,128)(2,1)S(1)} %get-tuple-element.25) | copy-start | bytes 4718596
  40.9 40.8 %copy-start.4 = (bf16[256,1024]{1,0:T(8,128)(2,1)}, bf16[256,1024]{1,0:T(8,128)(2,1)S(1)}, u32[]{:S(2)}) copy-start(bf16[256,1024]{1,0:T(8,128)(2,1)S(1)} %get-tuple-element.27) | copy-start | bytes 1572868
  42.9 1.3 copy-start.35
  44.2 0.5 copy-start.38
  70.6 1.2 copy-start.1
  71.8 1.7 copy-start.32
  72.6 1.6 copy-start.29
  72.6 3.6 %copy-start.41 = (pred[608]{0:T(1024)(128)(4,1)S(1)}, pred[608]{0:T(1024)(128)(4,1)}, u32[]{:S(2)}) copy-start(pred[608]{0:T(1024)(128)(4,1)} %copy-done.40) | copy-start | bytes 1828
  74.6 4.1 %copy-start.22 = (f32[1,608,256]{1,2,0:T(8,128)}, f32[1,608,256]{1,2,0:T(8,128)S(1)}, u32[]{:S(2)}) copy-start(f32[1,608,256]{1,2,0:T(8,128)S(1)} %copy.45) | copy-start | bytes 1867780
  76.2 1.6 copy-start.18
  77.8 2.6 copy-start.13
  81.6 25.8 %copy-start.25 = (bf16[4,64,608]{2,1,0:T(8,128)(2,1)}, bf16[4,64,608]{2,1,0:T(8,128)(2,1)S(1)}, u32[]{:S(2)}) copy-start(bf16[4,64,608]{2,1,0:T(8,128)(2,1)S(1)} %fusion.17) | copy-start | bytes 933892
  81.7 1.1 copy-start.6
  82.2 26.7 %copy-start.14 = (f32[152,1024]{1,0:T(8,128)S(1)}, f32[152,1024]{1,0:T(8,128)}, u32[]{:S(2)}) copy-start(f32[152,1024]{1,0:T(8,128)} %param.9) | copy-start | bytes 1867780
  82.2 26.7 %copy-start.34 = (f32[152]{0:T(256)S(1)}, f32[152]{0:T(256)}, u32[]{:S(2)}) copy-start(f32[152]{0:T(256)} %copy-done.33) | copy-start | bytes 1828
  107.5 1.3 copy-start.9
  108.8 1.5 copy-start.5
  109.2 77.8 %copy-start.16 = (f32[152,1024]{1,0:T(8,128)}, f32[152,1024]{1,0:T(8,128)S(1)}, u32[]{:S(2)}) copy-start(f32[152,1024]{1,0:T(8,128)S(1)} %get-tuple-element.93) | copy-start | bytes 1867780
  141.1 7.4 %copy-start.10 = (bf16[1024,1024]{1,0:T(8,128)(2,1)S(1)}, bf16[1024,1024]{1,0:T(8,128)(2,1)}, u32[]{:S(2)}) copy-start(bf16[1024,1024]{1,0:T(8,128)(2,1)} %copy-done.9) | copy-start | bytes 6291460
  186.6 1.1 copy-start.24
  187.9 0.9 copy-start.20
  216.6 1.3 copy-start
  217.8 6.4 %copy-start.2 = (bf16[4,152,1024]{2,1,0:T(8,128)(2,1)}, bf16[4,152,1024]{2,1,0:T(8,128)(2,1)S(1)}, u32[]{:S(2)}) copy-start(bf16[4,152,1024]{2,1,0:T(8,128)(2,1)S(1)} %get-tuple-element.36) | copy-start | bytes 3735556
  220.4 77.4 %collective-permute-start = (bf16[152,1024]{1,0:T(8,128)(2,1)}, bf16[152,1024]{1,0:T(8,128)(2,1)}, u32[]{:S(2)}, u32[]{:S(2)}) collective-permute-start(bf16[152,1024]{1,0:T(8,128)(2,1)} %get-tuple-element.96), channel_id=1, source_target_pairs={{0,1},{1,2},{2,3},{3,0},{4,5},{5,6},{6,7},{7,4},{8,9},{9,10},{10,1... | collective-permute-start | bytes 933896 | tf_op jit(solution)/shard_map/ppermute | solution.py:451
  220.4 77.4 %collective-permute-start.2 = (bf16[152,1024]{1,0:T(8,128)(2,1)}, bf16[152,1024]{1,0:T(8,128)(2,1)}, u32[]{:S(2)}, u32[]{:S(2)}) collective-permute-start(bf16[152,1024]{1,0:T(8,128)(2,1)} %get-tuple-element.97), channel_id=1, source_target_pairs={{0,3},{1,0},{2,1},{3,2},{4,7},{5,4},{6,5},{7,6},{8,11},{9,8},{10,9... | collective-permute-start | bytes 933896 | tf_op jit(solution)/shard_map/ppermute | solution.py:451
  224.2 73.5 %collective-permute-start.1 = (bf16[152,1024]{1,0:T(8,128)(2,1)}, bf16[152,1024]{1,0:T(8,128)(2,1)}, u32[]{:S(2)}, u32[]{:S(2)}) collective-permute-start(bf16[152,1024]{1,0:T(8,128)(2,1)} %get-tuple-element.98), channel_id=1, source_target_pairs={{0,2},{1,3},{2,0},{3,1},{4,6},{5,7},{6,4},{7,5},{8,10},{9,11},{10,... | collective-permute-start | bytes 933896 | tf_op jit(solution)/shard_map/ppermute | solution.py:451
  224.2 2.4 copy-start.26
  226.6 2.9 copy-start.31
  229.7 4.7 %copy-start.23 = (f32[1,608,256]{1,2,0:T(8,128)S(1)}, f32[1,608,256]{1,2,0:T(8,128)}, u32[]{:S(2)}) copy-start(f32[1,608,256]{1,2,0:T(8,128)} %copy-done.22) | copy-start | bytes 1867780
  229.7 9.1 %slice-start = ((s8[6225920]{0:T(1024)(128)(4,1)}), s8[4194304]{0:T(1024)(128)(4,1)S(1)}, s32[]{:S(2)}) async-start(s8[6225920]{0:T(1024)(128)(4,1)} %bitcast.104), calls=%async_computation | async-start | bytes 8388608
  234.4 4.4 %slice-start.1 = ((s8[6225920]{0:T(1024)(128)(4,1)}), s8[2031616]{0:T(1024)(128)(4,1)S(1)}, s32[]{:S(2)}) async-start(s8[6225920]{0:T(1024)(128)(4,1)} %bitcast.104), calls=%async_computation.1 | async-start | bytes 4063232
  238.8 1.3 copy-start.19
  242.0 1.4 copy-start.27
  242.0 2.7 copy-start.28
  245.6 4.6 %copy-start.12 = (bf16[3,1024,256]{2,1,0:T(8,128)(2,1)S(1)}, bf16[3,1024,256]{2,1,0:T(8,128)(2,1)}, u32[]{:S(2)}) copy-start(bf16[3,1024,256]{2,1,0:T(8,128)(2,1)} %copy-done.11) | copy-start | bytes 4718596
  245.6 4.6 %copy-start.30 = (bf16[1,608,256]{2,1,0:T(8,128)(2,1)S(1)}, bf16[1,608,256]{2,1,0:T(8,128)(2,1)}, u32[]{:S(2)}) copy-start(bf16[1,608,256]{2,1,0:T(8,128)(2,1)} %copy.54) | copy-start | bytes 933892
  259.4 1.3 copy-start.3
  289.4 8.3 %copy-start.15 = (f32[152,1024]{1,0:T(8,128)S(1)}, f32[152,1024]{1,0:T(8,128)}, u32[]{:S(2)}) copy-start(f32[152,1024]{1,0:T(8,128)} %param.9) | copy-start | bytes 1867780
  289.4 8.3 %copy-start.17 = (f32[152,1024]{1,0:T(8,128)S(1)}, f32[152,1024]{1,0:T(8,128)}, u32[]{:S(2)}) copy-start(f32[152,1024]{1,0:T(8,128)} %copy-done.16) | copy-start | bytes 1867780
  289.4 8.3 %copy-start.36 = (f32[152]{0:T(256)S(1)}, f32[152]{0:T(256)}, u32[]{:S(2)}) copy-start(f32[152]{0:T(256)} %copy-done.35) | copy-start | bytes 1828
  289.4 8.4 %copy-start.37 = (f32[152]{0:T(256)S(1)}, f32[152]{0:T(256)}, u32[]{:S(2)}) copy-start(f32[152]{0:T(256)} %fusion.25) | copy-start | bytes 1828
  297.8 14.8 %copy-start.39 = (f32[152]{0:T(256)S(1)}, f32[152]{0:T(256)}, u32[]{:S(2)}) copy-start(f32[152]{0:T(256)} %copy-done.38) | copy-start | bytes 1828
  300.7 12.9 %copy-start.21 = (f32[152,1024]{1,0:T(8,128)S(1)}, f32[152,1024]{1,0:T(8,128)}, u32[]{:S(2)}) copy-start(f32[152,1024]{1,0:T(8,128)} %copy-done.20) | copy-start | bytes 1867780
